TPU v7x, 512 devices: a whole 4x8x8 slice. The times are simulated.
512 devices in a mesh: dp: 64 (over y, z_hi, x), tensor: 8 (over z_lo, core).
Axes of the slice: x: 4, y: 8, z: 8 (z_hi: 2, z_lo: 4; z = z_hi * 4 + z_lo), core: 2. Of those that a mesh axis runs over, the one named last changes fastest.
Arguments:
- inputs: bfloat16 [8192, 4096], P('dp'), may hold values from -6 to 6
- w_key: bfloat16 [4096, 1024], P(None, 'tensor'), may hold values from -0.09375 to 0.09375
- values: bfloat16 [8192, 1024], P('dp', 'tensor'), may hold values from -6 to 6
- queries: bfloat16 [8192, 4096], P('dp', 'tensor'), may hold values from -200 to 200
- d_out: bfloat16 [8192, 4096], P('dp', 'tensor'), may hold values from -6 to 6
- doc_lens: int32 [4], replicated, may hold values from 1 to 4096, 8192 in all
- block_pos: int32 [128], P('dp'), may hold values from 0 to 127, as said below
Outputs:
- d_query: bfloat16 [8192, 4096], P('dp', 'tensor')
- d_value: bfloat16 [8192, 1024], P('dp', 'tensor')
- d_input: bfloat16 [8192, 4096], P('dp', 'tensor')
- d_wkey: float32 [4096, 1024], P('dp', 'tensor')
Inputs may be any that keep to these rules, and one draw needn't show every extreme that they name: `block_pos`: each stored block holds one block of 64 rows of the pack; every pack block is held once. `doc_lens`: lengths of the 4 documents in pack order; they sum to 8192.
All inputs are finite; a program needn't handle non-finite values.
Results may differ from a plain program's by a relative error of at most 0.023.
The roundings to bfloat16 on the way count: a program that leaves them out, or rounds other values in their place, can miss the bound.
Values may be sent and summed in bfloat16 or wider, within the bound.
A program may use at most 64 MiB of HBM per device.

v0:
```python
import math

import jax
import jax.numpy as jnp
from jax import lax
from jax.sharding import PartitionSpec as P

HD = 128
BLK = 64


masked_fill = -1e30


def row_positions(block_pos):
    within = jnp.tile(jnp.arange(BLK, dtype=jnp.int32), block_pos.shape[0])
    return jnp.repeat(block_pos, BLK) * BLK + within


def documents(positions, doc_lens):
    starts = jnp.cumsum(doc_lens) - doc_lens
    return jnp.sum((positions[:, None] >= starts[None, :]).astype(jnp.int32), axis=1) - 1


def split_heads(block_rows, kv_heads):
    return block_rows.reshape(block_rows.shape[0], kv_heads, HD)


def scored(query_heads, key_block, score_scale):
    key_split = split_heads(key_block, query_heads.shape[1])
    return (
        jnp.einsum("qcgd,kcd->cgqk", query_heads, key_split, preferred_element_type=jnp.float32)
        * score_scale
    )


def contributions(
    query_heads, grad_heads, key_block, value_block, allowed, row_max, row_sum, delta, score_scale
):
    kv_heads = query_heads.shape[1]
    key_split = split_heads(key_block, kv_heads)
    value_split = split_heads(value_block, kv_heads)
    scores = scored(query_heads, key_block, score_scale)
    mask_full = allowed[None, None]
    probabilities = (
        jnp.where(mask_full, jnp.exp(scores - row_max[..., None]), 0.0) / row_sum[..., None]
    )
    d_prob = jnp.einsum(
        "qcgd,kcd->cgqk", grad_heads, value_split, preferred_element_type=jnp.float32
    )
    d_score = probabilities * (d_prob - delta[..., None])
    prob_bf = probabilities.astype(jnp.bfloat16)
    score_bf = d_score.astype(jnp.bfloat16)
    query_part = score_scale * jnp.einsum(
        "cgqk,kcd->qcgd", score_bf, key_split, preferred_element_type=jnp.float32
    )
    key_part = score_scale * jnp.einsum(
        "cgqk,qcgd->kcd", score_bf, query_heads, preferred_element_type=jnp.float32
    )
    value_part = jnp.einsum(
        "cgqk,qcgd->kcd", prob_bf, grad_heads, preferred_element_type=jnp.float32
    )
    width_rows = key_block.shape[0]
    partial_value = jnp.concatenate(
        [key_part.reshape(width_rows, -1), value_part.reshape(width_rows, -1)], axis=1
    )
    return (query_part, partial_value)


def on_device(inputs, w_key, values, queries, d_out, doc_lens, block_pos):
    local_rows = inputs.shape[0]
    kv_heads = values.shape[1] // HD
    group_size = queries.shape[1] // (kv_heads * HD)
    kv_columns = kv_heads * HD
    score_scale = 1.0 / math.sqrt(HD)
    key_rows = jnp.dot(inputs, w_key, preferred_element_type=jnp.float32).astype(jnp.bfloat16)
    all_keys, all_values, all_blocks = (
        lax.all_gather(key_rows, "dp", axis=0, tiled=True),
        lax.all_gather(values, "dp", axis=0, tiled=True),
        lax.all_gather(block_pos, "dp", axis=0, tiled=True),
    )
    key_pos = row_positions(all_blocks)
    key_doc = documents(key_pos, doc_lens)
    query_pos = row_positions(block_pos)
    query_doc = documents(query_pos, doc_lens)
    query_heads = queries.reshape(local_rows, kv_heads, group_size, HD)
    grad_heads = d_out.reshape(local_rows, kv_heads, group_size, HD)
    total_rows = all_keys.shape[0]
    key_width = math.gcd(512, total_rows)
    stat_shape = (kv_heads, group_size, local_rows)

    def mask_for(first_row, width_rows):
        pos_here = lax.dynamic_slice_in_dim(key_pos, first_row, width_rows, 0)
        doc_here = lax.dynamic_slice_in_dim(key_doc, first_row, width_rows, 0)
        return (query_doc[:, None] == doc_here[None, :]) & (pos_here[None, :] <= query_pos[:, None])

    def visit_stats(block_index, running):
        first_row = block_index * key_width
        key_block = lax.dynamic_slice_in_dim(all_keys, first_row, key_width, 0)
        value_block = lax.dynamic_slice_in_dim(all_values, first_row, key_width, 0)
        allowed = mask_for(first_row, key_width)

        def visit_compute_live(state_now):
            row_max, row_sum, weighted = state_now
            scores = scored(query_heads, key_block, score_scale)
            mask_full = allowed[None, None]
            new_max = jnp.maximum(
                row_max, jnp.max(jnp.where(mask_full, scores, masked_fill), axis=3)
            )
            exp_terms = jnp.where(mask_full, jnp.exp(scores - new_max[..., None]), 0.0)
            d_prob = jnp.einsum(
                "qcgd,kcd->cgqk",
                grad_heads,
                split_heads(value_block, kv_heads),
                preferred_element_type=jnp.float32,
            )
            shrink = jnp.exp(row_max - new_max)
            return (
                new_max,
                row_sum * shrink + jnp.sum(exp_terms, axis=3),
                weighted * shrink + jnp.sum(exp_terms * d_prob, axis=3),
            )

        return lax.cond(jnp.any(allowed), visit_compute_live, lambda state_now: state_now, running)

    start_state = (
        jnp.full(stat_shape, masked_fill, jnp.float32),
        jnp.zeros(stat_shape, jnp.float32),
        jnp.zeros(stat_shape, jnp.float32),
    )
    row_max, row_sum, weighted = lax.fori_loop(0, total_rows // key_width, visit_stats, start_state)
    delta = weighted / row_sum

    def block_work(key_block, value_block, allowed):
        width_rows = key_block.shape[0]

        def block_compute_live(operands):
            return contributions(
                query_heads,
                grad_heads,
                operands[0],
                operands[1],
                operands[2],
                row_max,
                row_sum,
                delta,
                score_scale,
            )

        def dead_block(operands):
            return (
                jnp.zeros((local_rows, kv_heads, group_size, HD), jnp.float32),
                jnp.zeros((width_rows, 2 * kv_columns), jnp.float32),
            )

        return lax.cond(
            jnp.any(allowed), block_compute_live, dead_block, (key_block, value_block, allowed)
        )

    query_start = jnp.zeros((local_rows, kv_heads, group_size, HD), jnp.float32)

    def visit_block(block_index, running):
        query_sum, buffer_rows = running
        first_row = block_index * key_width
        key_block = lax.dynamic_slice_in_dim(all_keys, first_row, key_width, 0)
        value_block = lax.dynamic_slice_in_dim(all_values, first_row, key_width, 0)
        query_part, partial_value = block_work(
            key_block, value_block, mask_for(first_row, key_width)
        )
        return (
            query_sum + query_part,
            lax.dynamic_update_slice_in_dim(buffer_rows, partial_value, first_row, 0),
        )

    empty_buffer = jnp.zeros((total_rows, 2 * kv_columns), jnp.float32)
    query_sum, buffer_rows = lax.fori_loop(
        0, total_rows // key_width, visit_block, (query_start, empty_buffer)
    )
    arrived = lax.all_to_all(
        buffer_rows.astype(jnp.bfloat16), "dp", split_axis=0, concat_axis=0, tiled=True
    ).astype(buffer_rows.dtype)
    own_sums = jnp.sum(arrived.reshape(-1, local_rows, 2 * kv_columns), axis=0)
    d_query = query_sum.astype(jnp.bfloat16).reshape(local_rows, kv_columns * group_size)
    key_grad = own_sums[:, :kv_columns].astype(jnp.bfloat16)
    d_value = own_sums[:, kv_columns:].astype(jnp.bfloat16)
    d_wkey = lax.psum_scatter(
        lax.dot_general(
            inputs, key_grad, (((0,), (0,)), ((), ())), preferred_element_type=jnp.float32
        ),
        "dp",
        scatter_dimension=0,
        tiled=True,
    )
    partial_input = lax.dot_general(
        key_grad, w_key, (((1,), (1,)), ((), ())), preferred_element_type=jnp.float32
    )
    d_input = lax.psum_scatter(
        partial_input.astype(jnp.bfloat16), "tensor", scatter_dimension=1, tiled=True
    )
    return (d_query, d_value, d_input, d_wkey)


def solution(mesh):
    return jax.shard_map(
        on_device,
        mesh=mesh,
        in_specs=(
            P("dp", None),
            P(None, "tensor"),
            P("dp", "tensor"),
            P("dp", "tensor"),
            P("dp", "tensor"),
            P(),
            P("dp"),
        ),
        out_specs=(P("dp", "tensor"), P("dp", "tensor"), P("dp", "tensor"), P("dp", "tensor")),
        check_vma=False,
    )
```

profile of v0, /device:TPU:64, one launch (start us, length us, event | category | flops | bytes accessed | tf_op | source)
XLA Modules:
  0.0 1084.5 jit_solution(1409838610791566953)
XLA Ops:
  13.3 30.7 %all-reduce = s32[128]{0:T(128)S(1)} all-reduce(s32[128]{0:T(128)S(1)} %dynamic-update-slice), channel_id=1, replica_groups=mesh['dp'=64,'tensor'=8] {'dp'}, use_global_device_ids=true, to_apply=%add | all-reduce | flops 128 | bytes 1024
  45.0 109.7 %all-gather.5.cloned.1.call-done = bf16[8192,128]{1,0:T(8,128)(2,1)} async-done(((bf16[128,128]{1,0:T(8,128)(2,1)}), bf16[8192,128]{1,0:T(8,128)(2,1)}) %all-gather.5.cloned.1.call-update) | async-done | bytes 2097168 | tf_op jit(solution)/shard_map/all_gather | solution.py:79
  154.7 137.4 %all-gather.3.cloned.1.call-done = bf16[8192,128]{1,0:T(8,128)(2,1)} async-done(((bf16[128,128]{1,0:T(8,128)(2,1)}), bf16[8192,128]{1,0:T(8,128)(2,1)}) %all-gather.3.cloned.1.call-update) | async-done | bytes 2097168 | tf_op jit(solution)/shard_map/all_gather | solution.py:78
  292.0 73.1 %while.34 = (s32[]{:T(128)}, f32[1,4,128]{2,1,0:T(4,128)S(1)}, f32[1,4,128]{2,1,0:T(4,128)S(1)}, f32[1,4,128]{2,1,0:T(4,128)S(1)}, s32[128]{0:T(128)S(1)}, /*ind...) while((s32[]{:T(128)}, f32[1,4,128]{2,1,0:T(4,128)S(1)}, ...), condition=%wide.region_10.11_spmd.clone, body=%wide.region_3.10_spmd.clone.sunk | while | flops 137102976 | bytes 3985241 | solution.py:131
  367.4 113.4 %while.35 = (s32[]{:T(128)}, f32[128,1,4,128]{0,3,2,1:T(8,128)S(1)}, bf16[8192,256]{1,0:T(8,128)(2,1)}, s32[128]{0:T(128)S(1)}, s32[8192]{0:T(1024)S(1)}, /*inde...) while((s32[]{:T(128)}, ...), condition=%wide.region_15.16_spmd.clone, body=%wide.region_11.15_spmd.clone.sunk | while | flops 338755712 | bytes 8674131 | solution.py:176
  369.2 4.3 conditional.7
  376.3 4.3 conditional.7
  383.4 4.3 conditional.7
  390.5 4.3 conditional.7
  397.6 4.3 conditional.7
  404.7 4.3 conditional.7
  411.8 4.3 conditional.7
  418.9 4.3 conditional.7
  426.0 4.3 conditional.7
  433.0 4.3 conditional.7
  440.1 4.3 conditional.7
  447.2 4.3 conditional.7
  461.4 4.3 conditional.7
  468.5 4.3 conditional.7
  475.5 4.3 conditional.7
  480.8 6.4 copy.77
  487.2 102.2 %all_to_all.9 = bf16[64,128,256]{1,2,0:T(8,128)(2,1)} all-to-all(bf16[64,128,256]{1,2,0:T(8,128)(2,1)} %copy.77), channel_id=1, replica_groups=mesh['dp'=64,'tensor'=8] {'dp'}, dimensions={0} | all-to-all | bytes 8388608 | tf_op jit(solution)/shard_map/all_to_all | solution.py:179
  598.9 27.3 %reduce-scatter.5.cloned.1.call-done = bf16[128,512]{1,0:T(8,128)(2,1)} async-done(((bf16[128,4096]{1,0:T(8,128)(2,1)}), bf16[128,512]{1,0:T(8,128)(2,1)}) %reduce-scatter.5.cloned.1.call-update) | async-done | bytes 131088 | tf_op jit(solution)/shard_map/reduce_scatter | solution.py:197
  626.1 451.8 %reduce-scatter.7.cloned.1.call-done = f32[64,128]{1,0:T(8,128)} async-done(((f32[4096,128]{1,0:T(8,128)}), f32[64,128]{1,0:T(8,128)}) %reduce-scatter.7.cloned.1.call-update) | async-done | bytes 32784
  (472 shorter events, 229.3 us)
Async XLA Ops:
  7.2 1.2 copy-start
  7.2 3.6 copy-start.5
  7.2 3.8 copy-start.4
  7.2 36.9 %copy-start.2 = (bf16[128,512]{1,0:T(8,128)(2,1)S(1)}, bf16[128,512]{1,0:T(8,128)(2,1)}, u32[]{:S(2)}) copy-start(bf16[128,512]{1,0:T(8,128)(2,1)} %param.18) | copy-start | bytes 393220
  7.2 37.2 %copy-start.3 = (bf16[128,512]{1,0:T(8,128)(2,1)S(1)}, bf16[128,512]{1,0:T(8,128)(2,1)}, u32[]{:S(2)}) copy-start(bf16[128,512]{1,0:T(8,128)(2,1)} %param.19) | copy-start | bytes 393220
  7.2 147.4 %all-gather.5.cloned.1.call-start = ((), (), s32[]{:S(2)}) async-start(), calls=%async_computation.4 | async-start | bytes 2129920 | tf_op jit(solution)/shard_map/all_gather | solution.py:79
  8.0 284.1 %all-gather.3.cloned.1.call-start = ((), (), s32[]{:S(2)}) async-start(), calls=%async_computation.3 | async-start | bytes 2129920 | tf_op jit(solution)/shard_map/all_gather | solution.py:78
  10.7 615.4 %reduce-scatter.5.cloned.1.call-start = ((), (), s32[]{:S(2)}) async-start(), calls=%async_computation.5 | async-start | bytes 1179648 | tf_op jit(solution)/shard_map/reduce_scatter | solution.py:197
  592.2 3.2 copy-start.1
  593.7 484.2 %reduce-scatter.7.cloned.1.call-start = ((), (), s32[]{:S(2)}) async-start(), calls=%async_computation.6 | async-start | bytes 2129920
  597.3 0.8 slice-start
Sparse Core Ops, SparseCore 0:
  12.5 142.0 all-gather.4
  159.7 132.2 all-gather.2
  593.8 32.2 reduce-scatter.4
  629.3 448.5 reduce-scatter.6
where the time goes:
time: 1090 us; the launch traced here: 1080 us
  waiting for transfers between devices  727 us (67%)
  blocking collectives  133 us (12%)
  matrix products  113 us (10%)
  other arithmetic  37.6 us (3%)
  local copies, waits for them, and re-layouts  35.9 us (3%)
  loops' own time  23.4 us (2%)
  between operations  14.6 us (1%)
    unnamed x5, waiting for transfers between devices  453 us
    all_gather x1, waiting for transfers between devices, on_device(): lax.all_gather(key_rows, 'dp', axis=0, tiled=True)  137 us
    all_gather x1, waiting for transfers between devices, on_device(): lax.all_gather(values, 'dp', axis=0, tiled=True)  110 us
    all_to_all x1, blocking collectives, on_device(): lax.all_to_all(buffer_rows.astype(jnp.bfloat16), 'dp', split_axis=0, conc...  102 us
    dot_general x32, matrix products, scored(): jnp.einsum('qcgd,kcd->cgqk', query_heads, key_split, preferred_element_ty...  40.1 us
    unnamed x1, blocking collectives  30.7 us
    reduce_scatter x1, waiting for transfers between devices, on_device(): lax.psum_scatter(partial_input.astype(jnp.bfloat16), 'tensor', scatter_di...  27.3 us
  transfers between devices with their start and end apart: 4, of which 4 were waited for; matrix products, arithmetic and copies ran while one was open for 1% of the time, Pallas kernels for 0%

commit v1 on v0

v1 whole, which is shorter than its diff:
```python
import functools
import math

import jax
import jax.numpy as jnp
from jax import lax
from jax.experimental import pallas as pl
from jax.experimental.pallas import tpu as pltpu
from jax.sharding import PartitionSpec as P

MESH = pl.DeviceIdType.MESH
F32, BF16 = jnp.float32, jnp.bfloat16
HD, BLK, GROUP, ROWS = 128, 64, 4, 128
NX, NZ, NY, NC = 4, 2, 8, 2
HY, HX = NY // 2, NX // 2
KEY_BLOCKS = 2 * NZ * NY
QUERY_BLOCKS = 2 * NX
STACK = GROUP * BLK
CHUNK = 4
SCALE = 1.0 / math.sqrt(HD)
LOG2 = SCALE / math.log(2.0)
LOW = -1e30
FLOOR = -1e29
NT = (((1,), (1,)), ((), ()))
VMEM_LIMIT = 40 * 1024 * 1024

vmem = pl.BlockSpec(memory_space=pltpu.VMEM)
smem = pl.BlockSpec(memory_space=pltpu.SMEM)
anywhere = pl.BlockSpec(memory_space=pl.ANY)


def rem(a, n):
    return lax.rem(a, jnp.int32(n))


def place():
    dp, tensor = lax.axis_index("dp"), lax.axis_index("tensor")
    x = rem(dp, NX)
    rest = lax.div(dp, jnp.int32(NX))
    return lax.div(rest, jnp.int32(NZ)), rem(rest, NZ), x, tensor


def device(y, zh, x, tensor):
    return ((y * NZ + zh) * NX + x, tensor)


def meet(peers):
    barrier = pltpu.get_barrier_semaphore()
    for peer in peers:
        pl.semaphore_signal(barrier, inc=1, device_id=peer, device_id_type=MESH)
    pl.semaphore_wait(barrier, len(peers))


def send(src, dst, sems, index, peer):
    copy = pltpu.make_async_remote_copy(
        src_ref=src,
        dst_ref=dst,
        send_sem=sems[0].at[index],
        recv_sem=sems[1].at[index],
        device_id=peer,
        device_id_type=MESH,
    )
    copy.start()
    return copy


class Spread:
    def __init__(self, block, half, me, n, right, left, sems, base):
        self.block, self.half, self.me, self.n, self.h = block, half, me, n, n // 2
        self.right, self.left, self.sems, self.base = right, left, sems, base
        self.copies = []

    def step(self, s):
        if s > 1:
            for copy in self.copies[-1]:
                copy.wait_recv()
        pair = []
        for way, peer in enumerate((self.right, self.left)):
            shift = self.n - (s - 1) if way == 0 else s - 1
            ref = self.block(rem(self.me + shift, self.n))
            if s == self.h:
                ref = self.half(ref, way)
            pair.append(send(ref, ref, self.sems, self.base + 2 * (s - 1) + way, peer))
        self.copies.append(pair)

    def end(self):
        for copy in self.copies[-1]:
            copy.wait_recv()

    def drain(self):
        for pair in self.copies:
            for copy in pair:
                copy.wait_send()


class Reduce:
    def __init__(self, block, rows, me, n, right, left, got, made, sems, base):
        self.block, self.rows, self.me, self.n, self.h = block, rows, me, n, n // 2
        self.peers, self.got, self.made, self.sems, self.base = (right, left), got, made, sems, base
        self.copies = []

    def step(self, s):
        pair = []
        for way, peer in enumerate(self.peers):
            far = self.h - s + 1
            own = self.block(rem(self.me + (far if way == 0 else self.n - far), self.n))
            part = pl.ds(way * (self.rows // 2), self.rows // 2)
            other = pl.ds((1 - way) * (self.rows // 2), self.rows // 2)
            got, made = self.got[way], self.made[way]
            if s == 1:
                src, dst = own.at[part], got.at[0, part]
            else:
                self.copies[-1][way].wait_recv()
                out, before = made.at[s - 1], got.at[s - 2]
                if s == 2:
                    out[part] = (own[part].astype(F32) + before[part].astype(F32)).astype(BF16)
                    out[other] = own[other]
                else:
                    out[...] = (own[...].astype(F32) + before[...].astype(F32)).astype(BF16)
                src, dst = out, got.at[s - 1]
            pair.append(send(src, dst, self.sems, self.base + 2 * (s - 1) + way, peer))
        self.copies.append(pair)

    def total(self):
        for copy in self.copies[-1]:
            copy.wait_recv()
        last = self.h - 1
        return (
            self.block(self.me)[...].astype(F32)
            + self.got[0][last].astype(F32)
            + self.got[1][last].astype(F32)
        )

    def drain(self):
        for pair in self.copies:
            for copy in pair:
                copy.wait_send()


def gather_kernel(
    inputs, w_key, values, queries, d_out, block_pos, keys, vals, qs, gs, turned, places,
    x_buf, w_buf, y_send, y_recv, x_send, x_recv, z_send, z_recv, load_sem,
):
    y, zh, x, t = place()
    load_x = pltpu.make_async_copy(inputs, x_buf, load_sem.at[0])
    load_w = pltpu.make_async_copy(w_key, w_buf, load_sem.at[1])
    load_x.start()
    load_w.start()
    up, down = device(rem(y + 1, NY), zh, x, t), device(rem(y + NY - 1, NY), zh, x, t)
    right, left = device(y, zh, rem(x + 1, NX), t), device(y, zh, rem(x + NX - 1, NX), t)
    partner = device(y, 1 - zh, x, t)
    lane = lax.broadcasted_iota(jnp.int32, (16, ROWS), 1)
    first = 2 * (zh * NY + y)
    mine = jnp.where(lane == first, block_pos[0], 0) + jnp.where(lane == first + 1, block_pos[1], 0)
    seat = KEY_BLOCKS + 2 * x
    here = jnp.where(lane == seat, block_pos[0], 0) + jnp.where(lane == seat + 1, block_pos[1], 0)
    vals[zh, y, 0:ROWS, :] = values[...]
    vals[zh, y, ROWS : ROWS + 16, :] = mine.astype(F32).astype(BF16)
    qs[x] = queries[...]
    gs[x, 0:ROWS, :] = d_out[...]
    gs[x, ROWS : ROWS + 16, 0:HD] = here.astype(F32).astype(BF16)
    gs[x, ROWS : ROWS + 16, HD:] = jnp.zeros((16, (GROUP - 1) * HD), BF16)
    meet((up, down, right, left, partner))

    y_sems, x_sems, z_sems = (y_send, y_recv), (x_send, x_recv), (z_send, z_recv)

    def half_k(ref, way):
        return ref.at[pl.ds(way * 64, 64)]

    def half_v(ref, way):
        return ref.at[pl.ds(0, 64)] if way == 0 else ref.at[pl.ds(64, ROWS + 16 - 64)]

    def ring_y(arr, half, z, base):
        return Spread(lambda o: arr.at[z, o], half, y, NY, up, down, y_sems, base)

    v_own, v_far = ring_y(vals, half_v, zh, 0), ring_y(vals, half_v, 1 - zh, 2 * HY)
    k_own, k_far = ring_y(keys, half_k, zh, 4 * HY), ring_y(keys, half_k, 1 - zh, 6 * HY)
    q_ring = Spread(lambda o: qs.at[o], half_k, x, NX, right, left, x_sems, 0)
    g_ring = Spread(lambda o: gs.at[o], half_v, x, NX, right, left, x_sems, 2 * HX)

    z_v = send(vals.at[zh, y], vals.at[zh, y], z_sems, 0, partner)
    v_own.step(1)
    q_ring.step(1)
    g_ring.step(1)
    load_x.wait()
    load_w.wait()
    keys[zh, y] = jnp.dot(x_buf[...], w_buf[...], preferred_element_type=F32).astype(BF16)
    z_k = send(keys.at[zh, y], keys.at[zh, y], z_sems, 1, partner)
    k_own.step(1)

    def turn(first, last):
        def body(j, carry):
            tile = x_buf[:, pl.ds(pl.multiple_of(j * 128, 128), 128)].T
            for part in range(2):
                b = 2 * j + part
                turned[rem(b, NX), lax.div(b, jnp.int32(NX))] = tile[part * 64 : part * 64 + 64]
            return carry

        lax.fori_loop(first, last, body, 0)

    tiles = inputs.shape[1] // 128
    turn(0, tiles // 4)
    z_v.wait_recv()
    v_far.step(1)
    v_own.step(2)
    z_k.wait_recv()
    k_far.step(1)
    k_own.step(2)
    turn(tiles // 4, tiles // 2)
    q_ring.step(2)
    g_ring.step(2)
    v_far.step(2)
    k_far.step(2)
    v_own.step(3)
    k_own.step(3)
    turn(tiles // 2, 3 * tiles // 4)
    v_far.step(3)
    k_far.step(3)
    v_own.step(4)
    k_own.step(4)
    turn(3 * tiles // 4, tiles)
    v_far.step(4)
    k_far.step(4)
    rings = (v_own, k_own, v_far, k_far, q_ring, g_ring)
    for ring in rings:
        ring.end()
    total = jnp.zeros((16, ROWS), F32)
    for z in range(NZ):
        for j in range(NY):
            total = total + vals[z, j, ROWS : ROWS + 16, :].astype(F32)
    for j in range(NX):
        total = total + gs[j, ROWS : ROWS + 16, 0:HD].astype(F32)
    places[...] = total[0:8].astype(jnp.int32)
    z_v.wait_send()
    z_k.wait_send()
    for ring in rings:
        ring.drain()


def live_keys(places, doc_lens, listed, query):
    starts = [jnp.int32(0)]
    for d in range(3):
        starts.append(starts[-1] + doc_lens[d])
    mine = places[0, KEY_BLOCKS + query]
    first_row = mine * BLK
    start = jnp.int32(0)
    for s in starts[1:]:
        start = jnp.where(s <= first_row, s, start)
    low = lax.div(start, jnp.int32(BLK))
    count = jnp.int32(0)
    for b in range(KEY_BLOCKS):
        pk = places[0, b]
        listed[count] = jnp.int32(b)
        count = count + ((pk <= mine) & (pk >= low)).astype(jnp.int32)
    for j in range(CHUNK):
        listed[count + j] = jnp.int32(0)
    row = first_row + (lax.broadcasted_iota(jnp.int32, (1, 2 * BLK), 1) & (BLK - 1))
    opens = jnp.zeros((1, 2 * BLK), jnp.int32)
    for s in starts[1:]:
        opens = jnp.where(s <= row, s, opens)
    return count, row, opens


def key_chunk(places, listed, count, chunk, keys, vals, row, opens):
    iota = lax.broadcasted_iota(jnp.int32, (BLK, 2 * BLK), 0)
    ks, vs, terms, blocks = [], [], [], []
    for j in range(CHUNK):
        at = chunk * CHUNK + j
        b = listed[at]
        base = jnp.where(at < count, places[0, b] * BLK, jnp.int32(1 << 20))
        ks.append(keys[pl.ds(pl.multiple_of(b * BLK, BLK), BLK), :])
        vs.append(vals[b >> 1, pl.ds(pl.multiple_of((b & 1) * BLK, BLK), BLK), :])
        ok = (iota >= opens - base) & (iota <= row - base)
        term = jnp.where(ok, 0.0, LOW)
        terms.append(jnp.concatenate([term, term], axis=1))
        blocks.append(b)
    return (
        jnp.concatenate(ks, axis=0),
        jnp.concatenate(vs, axis=0),
        jnp.concatenate(terms, axis=0),
        blocks,
    )


def head_stack(ref, query):
    rows = pl.ds(pl.multiple_of((query & 1) * BLK, BLK), BLK)
    return jnp.concatenate(
        [ref[query >> 1, rows, h * HD : (h + 1) * HD] for h in range(GROUP)], axis=0
    )


def stats_kernel(places, doc_lens, keys, vals, qs, gs, out, kept, listed):
    def visit(query, carry):
        count, row, opens = live_keys(places, doc_lens, listed, query)
        q, g = head_stack(qs, query), head_stack(gs, query)

        def chunk_step(chunk, state):
            top, mass, weighted = state
            k, v, term, _ = key_chunk(places, listed, count, chunk, keys, vals, row, opens)
            score = lax.dot_general(k, q, NT, preferred_element_type=F32) * LOG2 + term
            d_prob = lax.dot_general(v, g, NT, preferred_element_type=F32)
            new = jnp.maximum(top, jnp.max(score, axis=0, keepdims=True))
            e = jnp.exp2(score - new)
            shrink = jnp.exp2(top - new)
            return (
                new,
                mass * shrink + jnp.sum(e, axis=0, keepdims=True),
                weighted * shrink + jnp.sum(e * d_prob, axis=0, keepdims=True),
            )

        zero = jnp.zeros((1, STACK), F32)
        chunks = lax.div(count + (CHUNK - 1), jnp.int32(CHUNK))
        top, mass, weighted = lax.fori_loop(
            0, chunks, chunk_step, (jnp.full((1, STACK), FLOOR, F32), zero, zero)
        )
        kept[query, 0:1] = top
        kept[query, 1:2] = mass
        kept[query, 2:3] = weighted
        return carry

    lax.fori_loop(0, QUERY_BLOCKS, visit, 0)
    for part in range(3):
        out[part] = jnp.concatenate([kept[i, part : part + 1] for i in range(QUERY_BLOCKS)], axis=0)


def share_kernel(stats, out, got, send_sem, recv_sem):
    y, zh, x, t = place()
    peers = [device(y, zh, rem(x + j, NX), t) for j in range(1, NX)]
    meet(peers)
    copies = [send(stats, got.at[j], (send_sem, recv_sem), j, peer) for j, peer in enumerate(peers)]
    for copy in copies:
        copy.wait_recv()
    parts = [[stats[i] for i in range(3)]] + [[got[j, i] for i in range(3)] for j in range(NX - 1)]
    top = parts[0][0]
    for p in parts[1:]:
        top = jnp.maximum(top, p[0])
    mass = jnp.zeros_like(top)
    weighted = jnp.zeros_like(top)
    for p in parts:
        shrink = jnp.exp2(p[0] - top)
        mass = mass + p[1] * shrink
        weighted = weighted + p[2] * shrink
    out[0] = top
    out[1] = 1.0 / mass
    out[2] = weighted / mass
    for copy in copies:
        copy.wait_send()


def back_kernel(
    places, doc_lens, stats, keys, vals, qs, gs, dq, dk, dv, dk_sum, dv_sum, listed
):
    dk_sum[...] = jnp.zeros_like(dk_sum)
    dv_sum[...] = jnp.zeros_like(dv_sum)

    def visit(query, carry):
        count, row, opens = live_keys(places, doc_lens, listed, query)
        q, g = head_stack(qs, query), head_stack(gs, query)
        top, scale, delta = [stats[i, pl.ds(query, 1), :] for i in range(3)]

        def chunk_step(chunk, dq_sum):
            k, v, term, blocks = key_chunk(places, listed, count, chunk, keys, vals, row, opens)
            score = lax.dot_general(k, q, NT, preferred_element_type=F32) * LOG2 + term
            d_prob = lax.dot_general(v, g, NT, preferred_element_type=F32)
            prob = jnp.exp2(score - top) * scale
            d_score = (prob * (d_prob - delta)).astype(BF16)
            dv_part = jnp.dot(prob.astype(BF16), g, preferred_element_type=F32)
            dk_part = jnp.dot(d_score, q, preferred_element_type=F32)
            for j, b in enumerate(blocks):
                rows = pl.ds(pl.multiple_of(b * BLK, BLK), BLK)
                dv_sum[rows, :] += dv_part[j * BLK : (j + 1) * BLK]
                dk_sum[rows, :] += dk_part[j * BLK : (j + 1) * BLK]
            return dq_sum + jnp.dot(k.T, d_score, preferred_element_type=F32)

        chunks = lax.div(count + (CHUNK - 1), jnp.int32(CHUNK))
        dq_sum = lax.fori_loop(0, chunks, chunk_step, jnp.zeros((HD, STACK), F32))
        dq_rows = (dq_sum * SCALE).T.astype(BF16)
        rows = pl.ds(pl.multiple_of((query & 1) * BLK, BLK), BLK)
        for h in range(GROUP):
            dq[query >> 1, rows, h * HD : (h + 1) * HD] = dq_rows[h * BLK : (h + 1) * BLK]
        return carry

    lax.fori_loop(0, QUERY_BLOCKS, visit, 0)
    dk[...] = (dk_sum[...] * SCALE).astype(BF16)
    dv[...] = dv_sum[...].astype(BF16)


def reduce_kernel(
    nl, dq, dk, dv, turned, w_key, d_query, d_value, d_input, d_wkey,
    kv_got, kv_made, q_got, q_made, w_got, w_made, z_out, z_got, kg, kg_pair, xg, x_hop, w_own, w_pair,
    w_part, in_part, in_got, zw_out, zw_got,
    y_send, y_recv, x_send, x_recv, z_send, z_recv, s_send, s_recv, load_sem,
):
    y, zh, x, t = place()
    zl, core = lax.div(t, jnp.int32(NC)), rem(t, NC)
    up, down = device(rem(y + 1, NY), zh, x, t), device(rem(y + NY - 1, NY), zh, x, t)
    others_x = [device(y, zh, rem(x + j, NX), t) for j in range(1, NX)]
    right, left = others_x[0], others_x[-1]
    partner = device(y, 1 - zh, x, t)
    sibling = device(y, zh, x, zl * NC + 1 - core)
    others_l = [device(y, zh, x, rem(zl + j, nl) * NC + core) for j in range(1, nl)]
    x_sems, y_sems = (x_send, x_recv), (y_send, y_recv)
    z_sems, s_sems = (z_send, z_recv), (s_send, s_recv)

    own_x = pltpu.make_async_copy(turned.at[x], xg.at[x], load_sem.at[0])
    own_w = pltpu.make_async_copy(w_key.at[:, core], w_own, load_sem.at[1])
    own_x.start()
    own_w.start()
    meet([up, down, partner, sibling] + others_x + others_l)

    def ring(arr, z, j):
        return Reduce(
            lambda o: arr.at[z, o], ROWS, y, NY, up, down,
            (kv_got.at[j, 0], kv_got.at[j, 1]), (kv_made.at[j, 0], kv_made.at[j, 1]),
            y_sems, 2 * HY * j,
        )

    k_far, v_far = ring(dk, 1 - zh, 0), ring(dv, 1 - zh, 1)
    k_own, v_own = ring(dk, zh, 2), ring(dv, zh, 3)
    rings = (k_far, k_own, v_far, v_own)
    for r in rings:
        r.step(1)
    pairs = NZ * NY
    opposite = rem(x + 2, NX)
    x_next = send(turned.at[rem(x + 1, NX)], xg.at[x], x_sems, 0, right)
    x_prev = send(turned.at[rem(x + NX - 1, NX)], xg.at[x], x_sems, 1, left)
    lower, upper = pl.ds(0, pairs // 2), pl.ds(pairs // 2, pairs // 2)
    hop_right = send(turned.at[opposite, lower], x_hop.at[0], x_sems, 2, right)
    hop_left = send(turned.at[opposite, upper], x_hop.at[1], x_sems, 3, left)
    w_swap = send(w_key.at[:, 1 - core], w_pair, s_sems, 0, sibling)
    q_ring = Reduce(
        lambda o: dq.at[o], ROWS, x, NX, right, left,
        (q_got.at[0], q_got.at[1]), (q_made.at[0], q_made.at[1]), x_sems, 4,
    )
    q_ring.step(1)
    for r in rings:
        r.step(2)
    hop_right.wait_recv()
    far_right = send(x_hop.at[0], xg.at[rem(x + NX - 1, NX), lower], x_sems, 8, right)
    hop_left.wait_recv()
    far_left = send(x_hop.at[1], xg.at[rem(x + 1, NX), upper], x_sems, 9, left)
    for r in rings:
        r.step(3)
    q_ring.step(2)
    for r in rings:
        r.step(4)
    z_out[0] = k_far.total().astype(BF16)
    z_key = send(z_out.at[0], z_got.at[0], z_sems, 0, partner)
    key_sum = k_own.total()
    z_out[1] = v_far.total().astype(BF16)
    z_val = send(z_out.at[1], z_got.at[1], z_sems, 1, partner)
    z_key.wait_recv()
    kg[x] = (key_sum + z_got[0].astype(F32)).astype(BF16)

    kg_swap = send(kg.at[x], kg_pair, s_sems, 1, sibling)
    kg_sends = [send(kg.at[x], kg.at[x], x_sems, 9 + j, others_x[j - 1]) for j in range(1, NX)]

    own_w.wait()
    w_swap.wait_recv()
    kg_swap.wait_recv()
    in_sends = []
    mine, pair = kg[x], kg_pair[...]

    def in_block(owner):
        return lax.dot_general(
            mine, w_own[owner], NT, preferred_element_type=F32
        ) + lax.dot_general(pair, w_pair[owner], NT, preferred_element_type=F32)

    for j in range(1, nl):
        in_part[j - 1] = in_block(rem(zl + j, nl)).astype(BF16)
        in_sends.append(send(in_part.at[j - 1], in_got.at[j - 1], s_sems, 1 + j, others_l[j - 1]))

    own_x.wait()
    x_next.wait_recv()
    x_prev.wait_recv()
    far_right.wait_recv()
    far_left.wait_recv()
    for copy in kg_sends:
        copy.wait_recv()
    product = jnp.zeros((pairs * BLK, HD), F32)
    for src in range(NX):
        block = xg[src].reshape(pairs * BLK, ROWS)
        product = product + jnp.dot(block, kg[src], preferred_element_type=F32)
    w_part[...] = product.astype(BF16).reshape(NY, NZ * BLK, HD)
    w_ring = Reduce(
        lambda o: w_part.at[o], NZ * BLK, y, NY, up, down,
        (w_got.at[0], w_got.at[1]), (w_made.at[0], w_made.at[1]), y_sems, 8 * HY,
    )
    w_ring.step(1)
    z_val.wait_recv()
    d_value[...] = (v_own.total() + z_got[1].astype(F32)).astype(BF16)
    w_ring.step(2)
    d_query[...] = q_ring.total().astype(BF16)
    w_ring.step(3)
    in_sum = in_block(zl)
    w_ring.step(4)
    zw_out[...] = w_ring.total()
    z_w = send(
        zw_out.at[pl.ds(pl.multiple_of((1 - zh) * BLK, BLK), BLK)], zw_got, z_sems, 2, partner
    )
    for j, copy in enumerate(in_sends):
        copy.wait_recv()
        in_sum = in_sum + in_got[j].astype(F32)
    d_input[...] = in_sum.astype(BF16)
    z_w.wait_recv()
    d_wkey[...] = zw_out[pl.ds(pl.multiple_of(zh * BLK, BLK), BLK), :] + zw_got[...]

    for r in rings + (q_ring, w_ring):
        r.drain()
    last = [x_next, x_prev, hop_right, hop_left, far_right, far_left, w_swap, z_key, z_val, kg_swap, z_w]
    for copy in last + kg_sends + in_sends:
        copy.wait_send()


def dma(n):
    return pltpu.SemaphoreType.DMA((n,))


def params(collective_id=None):
    return pltpu.CompilerParams(
        collective_id=collective_id,
        has_side_effects=collective_id is not None,
        vmem_limit_bytes=VMEM_LIMIT,
    )


def on_device(nl, inputs, w_key, values, queries, d_out, doc_lens, block_pos):
    width = inputs.shape[1]
    pairs = NZ * NY
    shape = jax.ShapeDtypeStruct
    keys, vals, qs, gs, turned, places = pl.pallas_call(
        gather_kernel,
        out_shape=(
            shape((NZ, NY, ROWS, HD), BF16),
            shape((NZ, NY, ROWS + 16, HD), BF16),
            shape((NX, ROWS, GROUP * HD), BF16),
            shape((NX, ROWS + 16, GROUP * HD), BF16),
            shape((NX, pairs, BLK, ROWS), BF16),
            shape((8, ROWS), jnp.int32),
        ),
        in_specs=[anywhere, anywhere, vmem, vmem, vmem, smem],
        out_specs=(vmem,) * 6,
        scratch_shapes=[
            pltpu.VMEM((ROWS, width), BF16),
            pltpu.VMEM((width, HD), BF16),
            dma(8 * HY), dma(8 * HY), dma(4 * HX), dma(4 * HX), dma(2), dma(2), dma(2),
        ],
        compiler_params=params(1),
        name="gather_rows",
    )(inputs, w_key, values, queries, d_out, block_pos)
    keys = keys.reshape(KEY_BLOCKS * BLK, HD)
    vals = vals.reshape(pairs, ROWS + 16, HD)
    stats = pl.pallas_call(
        stats_kernel,
        out_shape=shape((3, QUERY_BLOCKS, STACK), F32),
        in_specs=[smem, smem, vmem, vmem, vmem, vmem],
        out_specs=vmem,
        scratch_shapes=[
            pltpu.VMEM((QUERY_BLOCKS, 8, STACK), F32),
            pltpu.SMEM((KEY_BLOCKS + CHUNK,), jnp.int32),
        ],
        compiler_params=params(),
        name="row_stats",
    )(places, doc_lens, keys, vals, qs, gs)
    stats = pl.pallas_call(
        share_kernel,
        out_shape=shape((3, QUERY_BLOCKS, STACK), F32),
        in_specs=[vmem],
        out_specs=vmem,
        scratch_shapes=[
            pltpu.VMEM((NX - 1, 3, QUERY_BLOCKS, STACK), F32), dma(NX - 1), dma(NX - 1),
        ],
        compiler_params=params(2),
        name="share_stats",
    )(stats)
    dq, dk, dv = pl.pallas_call(
        back_kernel,
        out_shape=(
            shape((NX, ROWS, GROUP * HD), BF16),
            shape((KEY_BLOCKS * BLK, HD), BF16),
            shape((KEY_BLOCKS * BLK, HD), BF16),
        ),
        in_specs=[smem, smem, vmem, vmem, vmem, vmem, vmem],
        out_specs=(vmem,) * 3,
        scratch_shapes=[
            pltpu.VMEM((KEY_BLOCKS * BLK, HD), F32),
            pltpu.VMEM((KEY_BLOCKS * BLK, HD), F32),
            pltpu.SMEM((KEY_BLOCKS + CHUNK,), jnp.int32),
        ],
        compiler_params=params(),
        name="back_tiles",
    )(places, doc_lens, stats, keys, vals, qs, gs)
    slice_width = width // (nl * NC)
    w_split = w_key.reshape(nl, NC, slice_width, HD)
    block = (ROWS, HD)
    return pl.pallas_call(
        functools.partial(reduce_kernel, nl),
        out_shape=(
            shape((ROWS, GROUP * HD), BF16),
            shape((ROWS, HD), BF16),
            shape((ROWS, slice_width), BF16),
            shape((BLK, HD), F32),
        ),
        in_specs=[vmem, vmem, vmem, anywhere, anywhere],
        out_specs=(vmem,) * 4,
        scratch_shapes=[
            pltpu.VMEM((4, 2, HY) + block, BF16),
            pltpu.VMEM((4, 2, HY) + block, BF16),
            pltpu.VMEM((2, HX, ROWS, GROUP * HD), BF16),
            pltpu.VMEM((2, HX, ROWS, GROUP * HD), BF16),
            pltpu.VMEM((2, HY) + block, BF16),
            pltpu.VMEM((2, HY) + block, BF16),
            pltpu.VMEM((2,) + block, BF16),
            pltpu.VMEM((2,) + block, BF16),
            pltpu.VMEM((NX,) + block, BF16),
            pltpu.VMEM(block, BF16),
            pltpu.VMEM((NX, pairs, BLK, ROWS), BF16),
            pltpu.VMEM((2, pairs // 2, BLK, ROWS), BF16),
            pltpu.VMEM((nl, slice_width, HD), BF16),
            pltpu.VMEM((nl, slice_width, HD), BF16),
            pltpu.VMEM((NY,) + block, BF16),
            pltpu.VMEM((nl - 1, ROWS, slice_width), BF16),
            pltpu.VMEM((nl - 1, ROWS, slice_width), BF16),
            pltpu.VMEM(block, F32),
            pltpu.VMEM((BLK, HD), F32),
            dma(10 * HY), dma(10 * HY), dma(13), dma(13), dma(3), dma(3), dma(1 + nl), dma(1 + nl), dma(2),
        ],
        compiler_params=params(3),
        name="reduce_grads",
    )(dq, dk.reshape(NZ, NY, ROWS, HD), dv.reshape(NZ, NY, ROWS, HD), turned, w_split)


def solution(mesh):
    nl = mesh.shape["tensor"] // NC
    return jax.shard_map(
        functools.partial(on_device, nl),
        mesh=mesh,
        in_specs=(
            P("dp", None),
            P(None, "tensor"),
            P("dp", "tensor"),
            P("dp", "tensor"),
            P("dp", "tensor"),
            P(),
            P("dp"),
        ),
        out_specs=(P("dp", "tensor"), P("dp", "tensor"), P("dp", "tensor"), P("dp", "tensor")),
        check_vma=False,
    )
```

time: 1090 us -> 121 us (0.11)
  the two profiles are of different devices: /device:TPU:64 before, /device:TPU:8 now
where the time goes in v1:
time: 121 us; the launch traced here: 120 us
  Pallas kernels  111 us (92%)
  local copies, waits for them, and re-layouts  8.86 us (7%)
    pallas_call x1, Pallas kernels, on_device(): pl.pallas_call(functools.partial(reduce_kernel, nl), out_shape=(shape((RO...  54.8 us
    pallas_call x1, Pallas kernels, on_device(): pl.pallas_call(gather_kernel, out_shape=(shape((NZ, NY, ROWS, HD), BF16),...  33.6 us
    pallas_call x1, Pallas kernels, on_device(): pl.pallas_call(back_kernel, out_shape=(shape((NX, ROWS, GROUP * HD), BF16...  9.52 us
    unnamed x20, local copies, waits for them, and re-layouts  8.86 us
    pallas_call x1, Pallas kernels, on_device(): pl.pallas_call(share_kernel, out_shape=shape((3, QUERY_BLOCKS, STACK), F3...  6.4 us
    pallas_call x1, Pallas kernels, on_device(): pl.pallas_call(stats_kernel, out_shape=shape((3, QUERY_BLOCKS, STACK), F3...  6.29 us

profile of v1, /device:TPU:8, one launch (start us, length us, event | category | flops | bytes accessed | tf_op | source)
XLA Modules:
  0.0 120.2 jit_solution(648266759007286025)
XLA Ops:
  0.6 0.0 copy-start.7
  0.6 0.6 copy-done.7
  1.3 0.0 copy-start
  1.3 1.2 %copy-done = bf16[4096,128]{1,0:T(8,128)(2,1)S(1)} copy-done((bf16[4096,128]{1,0:T(8,128)(2,1)S(1)}, bf16[4096,128]{1,0:T(8,128)(2,1)}, u32[]{:S(2)}) %copy-start) | copy-done | bytes 1048600
  2.5 0.0 copy-start.2
  2.5 1.2 %copy-done.2 = bf16[128,4096]{1,0:T(8,128)(2,1)S(1)} copy-done((bf16[128,4096]{1,0:T(8,128)(2,1)S(1)}, bf16[128,4096]{1,0:T(8,128)(2,1)}, u32[]{:S(2)}) %copy-start.2) | copy-done | bytes 1048600
  3.7 0.0 copy-start.3
  3.7 0.9 copy-done.3
  4.6 0.0 copy-start.4
  4.6 0.9 copy-done.4
  5.6 0.8 copy-done.5
  6.3 33.6 %gather_rows.1 = (bf16[2,8,128,128]{3,2,1,0:T(8,128)(2,1)S(1)}, bf16[2,8,144,128]{3,2,1,0:T(8,128)(2,1)S(1)}, bf16[4,128,512]{2,1,0:T(8,128)(2,1)S(1)}, bf16[4,1...) custom-call(bf16[128,4096]{1,0:T(8,128)(2,1)S(1)} %copy-done.2, ...), custom_call_target="tpu_custom_call" | custom-call | tf_op jit(solution)/shard_map/gather_rows/pallas_call | solution.py:531
  40.0 0.0 copy-start.6
  40.0 0.6 copy-done.6
  40.6 6.3 %row_stats.1.stats = f32[3,8,256]{2,1,0:T(8,128)S(1)} custom-call(s32[8,128]{1,0:T(8,128)S(1)} %get-tuple-element.13.places, s32[4]{0:T(128)S(1)} %copy-done.6, bf16[2048,128]{1,0:T(8,128)(2,1)S(1)} %bitcast.8, bf16[16,144,128]{2,1,0:T(8,128)(2,1)S(1)} %bitcast.6, bf16[4,128,512]{2,1,0:T(8,128)(2,1)S(1)} %get-tuple-element.16.qs, ...), custom_call_target="tpu_custom_call" | custom-call | tf_op jit(solution)/shard_map/row_stats/pallas_call | solution.py:553
  46.9 6.4 %share_stats.1.stats = f32[3,8,256]{2,1,0:T(8,128)S(1)} custom-call(f32[3,8,256]{2,1,0:T(8,128)S(1)} %row_stats.1.stats), custom_call_target="tpu_custom_call" | custom-call | tf_op jit(solution)/shard_map/share_stats/pallas_call | solution.py:565
  53.3 0.0 copy-start.1
  53.3 9.5 %back_tiles.1 = (bf16[4,128,512]{2,1,0:T(8,128)(2,1)S(1)}, bf16[2048,128]{1,0:T(8,128)(2,1)S(1)}, bf16[2048,128]{1,0:T(8,128)(2,1)S(1)}) custom-call(s32[8,128]{1,0:T(8,128)S(1)} %get-tuple-element.13.places, s32[4]{0:T(128)S(1)} %copy-done.6, f32[3,8,256]{2,1,0:T(8,128)S(1)} %share_stats.1.stats, bf16[2048,128]{1,0:T(8,128)(2,1)S(1)} %bitcast.9, ...), custom_call_target="tpu_custom_call" | custom-call | tf_op jit(solution)/shard_map/back_tiles/pallas_call | solution.py:576
  62.9 0.0 copy-done.1
  62.9 54.8 %reduce_grads.1 = (bf16[128,512]{1,0:T(8,128)(2,1)S(1)}, bf16[128,128]{1,0:T(8,128)(2,1)S(1)}, bf16[128,512]{1,0:T(8,128)(2,1)S(1)}, f32[64,128]{1,0:T(8,128)S(1)}) custom-call(bf16[4,128,512]{2,1,0:T(8,128)(2,1)S(1)} %get-tuple-element.18.dq, bf16[2,8,128,128]{3,2,1,0:T(8,128)(2,1)S(1)} %bitcast.10, bf16[2,8,128,128]{3,2,1,0:T(8,128)(2,1)S(1)} %bitcast.11, ...), custom_call_target="tpu_custom_call" | custom-call | tf_op jit(solution)/shard_map/reduce_grads/pallas_call | solution.py:596
  117.6 0.7 copy.15
  118.3 0.6 copy.16
  118.9 0.7 copy.17
  119.6 0.6 copy.18
  (1 shorter events, 0.0 us)
Async XLA Ops:
  0.6 0.7 copy-start.7
  1.3 1.2 %copy-start = (bf16[4096,128]{1,0:T(8,128)(2,1)S(1)}, bf16[4096,128]{1,0:T(8,128)(2,1)}, u32[]{:S(2)}) copy-start(bf16[4096,128]{1,0:T(8,128)(2,1)} %w_key.1) | copy-start | bytes 3145732
  2.5 1.2 %copy-start.2 = (bf16[128,4096]{1,0:T(8,128)(2,1)S(1)}, bf16[128,4096]{1,0:T(8,128)(2,1)}, u32[]{:S(2)}) copy-start(bf16[128,4096]{1,0:T(8,128)(2,1)} %inputs.1) | copy-start | bytes 3145732
  3.7 0.9 copy-start.3
  4.6 0.9 copy-start.4
  5.5 0.8 copy-start.5
  40.0 0.7 copy-start.6
  53.3 9.5 %copy-start.1 = (bf16[4096,128]{1,0:T(8,128)(2,1)S(1)}, bf16[4096,128]{1,0:T(8,128)(2,1)}, u32[]{:S(2)}) copy-start(bf16[4096,128]{1,0:T(8,128)(2,1)} %w_key.1) | copy-start | bytes 3145732

commit v2 on v1

--- a/solution.py
+++ b/solution.py
@@ -26,7 +26,7 @@
 
 vmem = pl.BlockSpec(memory_space=pltpu.VMEM)
 smem = pl.BlockSpec(memory_space=pltpu.SMEM)
-anywhere = pl.BlockSpec(memory_space=pl.ANY)
+hbm = pl.BlockSpec(memory_space=pltpu.HBM)
 
 
 def rem(a, n):
@@ -121,14 +121,16 @@
             pair.append(send(src, dst, self.sems, self.base + 2 * (s - 1) + way, peer))
         self.copies.append(pair)
 
-    def total(self):
+    def end(self):
         for copy in self.copies[-1]:
             copy.wait_recv()
+
+    def total(self, z):
         last = self.h - 1
         return (
-            self.block(self.me)[...].astype(F32)
-            + self.got[0][last].astype(F32)
-            + self.got[1][last].astype(F32)
+            self.block(self.me)[z].astype(F32)
+            + self.got[0][last, z].astype(F32)
+            + self.got[1][last, z].astype(F32)
         )
 
     def drain(self):
@@ -137,30 +139,72 @@
                 copy.wait_send()
 
 
+class Tree:
+    def __init__(self, block, half, me, n, ups, downs, sems, base):
+        self.block, self.half, self.me, self.n = block, half, me, n
+        self.ups, self.downs, self.sems, self.base = ups, downs, sems, base
+
+    def first(self):
+        own = self.block(self.me)
+        self.near = [
+            send(own, own, self.sems, self.base + i, peer)
+            for i, peer in enumerate((self.ups[1], self.downs[1], self.ups[0], self.downs[0]))
+        ]
+
+    def second(self):
+        self.far = []
+        for way, peers in enumerate((self.ups, self.downs)):
+            self.near[way].wait_recv()
+            ref = self.block(rem(self.me + (self.n - 2 if way == 0 else 2), self.n))
+            half = self.half(ref, way)
+            self.far.append(send(half, half, self.sems, self.base + 4 + 2 * way, peers[1]))
+            self.far.append(send(ref, ref, self.sems, self.base + 5 + 2 * way, peers[0]))
+
+    def end(self):
+        for copy in self.near[2:] + self.far:
+            copy.wait_recv()
+
+    def drain(self):
+        for copy in self.near + self.far:
+            copy.wait_send()
+
+
 def gather_kernel(
-    inputs, w_key, values, queries, d_out, block_pos, keys, vals, qs, gs, turned, places,
-    x_buf, w_buf, y_send, y_recv, x_send, x_recv, z_send, z_recv, load_sem,
+    inputs, w_key, values, queries, d_out, doc_lens, block_pos, keys, vals, qs, gs, turned, places,
+    x_buf, w_buf, docs, pos, y_send, y_recv, x_send, x_recv, z_send, z_recv, load_sem,
 ):
     y, zh, x, t = place()
-    load_x = pltpu.make_async_copy(inputs, x_buf, load_sem.at[0])
-    load_w = pltpu.make_async_copy(w_key, w_buf, load_sem.at[1])
-    load_x.start()
-    load_w.start()
-    up, down = device(rem(y + 1, NY), zh, x, t), device(rem(y + NY - 1, NY), zh, x, t)
-    right, left = device(y, zh, rem(x + 1, NX), t), device(y, zh, rem(x + NX - 1, NX), t)
+    loads = [
+        pltpu.make_async_copy(src, dst, load_sem.at[i])
+        for i, (src, dst) in enumerate(
+            (
+                (block_pos, pos),
+                (values, vals.at[zh, y, pl.ds(0, ROWS)]),
+                (queries, qs.at[x]),
+                (d_out, gs.at[x, pl.ds(0, ROWS)]),
+                (w_key, w_buf),
+                (inputs, x_buf),
+                (doc_lens, docs),
+            )
+        )
+    ]
+    for load in loads:
+        load.start()
+    ups = [device(rem(y + j, NY), zh, x, t) for j in (1, 2)]
+    downs = [device(rem(y + NY - j, NY), zh, x, t) for j in (1, 2)]
+    others_x = [device(y, zh, rem(x + j, NX), t) for j in range(1, NX)]
     partner = device(y, 1 - zh, x, t)
+    loads[0].wait()
     lane = lax.broadcasted_iota(jnp.int32, (16, ROWS), 1)
     first = 2 * (zh * NY + y)
-    mine = jnp.where(lane == first, block_pos[0], 0) + jnp.where(lane == first + 1, block_pos[1], 0)
+    mine = jnp.where(lane == first, pos[0], 0) + jnp.where(lane == first + 1, pos[1], 0)
     seat = KEY_BLOCKS + 2 * x
-    here = jnp.where(lane == seat, block_pos[0], 0) + jnp.where(lane == seat + 1, block_pos[1], 0)
-    vals[zh, y, 0:ROWS, :] = values[...]
+    here = jnp.where(lane == seat, pos[0], 0) + jnp.where(lane == seat + 1, pos[1], 0)
     vals[zh, y, ROWS : ROWS + 16, :] = mine.astype(F32).astype(BF16)
-    qs[x] = queries[...]
-    gs[x, 0:ROWS, :] = d_out[...]
     gs[x, ROWS : ROWS + 16, 0:HD] = here.astype(F32).astype(BF16)
     gs[x, ROWS : ROWS + 16, HD:] = jnp.zeros((16, (GROUP - 1) * HD), BF16)
-    meet((up, down, right, left, partner))
+    loads[1].wait()
+    meet(ups + downs + others_x + [partner])
 
     y_sems, x_sems, z_sems = (y_send, y_recv), (x_send, x_recv), (z_send, z_recv)
 
@@ -170,23 +214,28 @@
     def half_v(ref, way):
         return ref.at[pl.ds(0, 64)] if way == 0 else ref.at[pl.ds(64, ROWS + 16 - 64)]
 
-    def ring_y(arr, half, z, base):
-        return Spread(lambda o: arr.at[z, o], half, y, NY, up, down, y_sems, base)
-
-    v_own, v_far = ring_y(vals, half_v, zh, 0), ring_y(vals, half_v, 1 - zh, 2 * HY)
-    k_own, k_far = ring_y(keys, half_k, zh, 4 * HY), ring_y(keys, half_k, 1 - zh, 6 * HY)
-    q_ring = Spread(lambda o: qs.at[o], half_k, x, NX, right, left, x_sems, 0)
-    g_ring = Spread(lambda o: gs.at[o], half_v, x, NX, right, left, x_sems, 2 * HX)
+    def ring(arr, half, base):
+        return Spread(lambda o: arr.at[zh, o], half, y, NY, ups[0], downs[0], y_sems, base)
+
+    def tree(arr, half, base):
+        return Tree(lambda o: arr.at[1 - zh, o], half, y, NY, ups, downs, y_sems, base)
+
+    v_own, k_own = ring(vals, half_v, 0), ring(keys, half_k, 8)
+    v_far, k_far = tree(vals, half_v, 16), tree(keys, half_k, 24)
 
     z_v = send(vals.at[zh, y], vals.at[zh, y], z_sems, 0, partner)
     v_own.step(1)
-    q_ring.step(1)
-    g_ring.step(1)
-    load_x.wait()
-    load_w.wait()
+    loads[4].wait()
+    loads[5].wait()
     keys[zh, y] = jnp.dot(x_buf[...], w_buf[...], preferred_element_type=F32).astype(BF16)
     z_k = send(keys.at[zh, y], keys.at[zh, y], z_sems, 1, partner)
     k_own.step(1)
+    loads[2].wait()
+    loads[3].wait()
+    sideways = []
+    for j in (2, 1, 3):
+        sideways.append(send(gs.at[x], gs.at[x], x_sems, j - 1, others_x[j - 1]))
+        sideways.append(send(qs.at[x], qs.at[x], x_sems, j + 2, others_x[j - 1]))
 
     def turn(first, last):
         def body(j, carry):
@@ -200,47 +249,50 @@
 
     tiles = inputs.shape[1] // 128
     turn(0, tiles // 4)
+    v_own.step(2)
+    k_own.step(2)
     z_v.wait_recv()
-    v_far.step(1)
-    v_own.step(2)
+    v_far.first()
+    v_own.step(3)
     z_k.wait_recv()
-    k_far.step(1)
-    k_own.step(2)
+    k_far.first()
+    k_own.step(3)
     turn(tiles // 4, tiles // 2)
-    q_ring.step(2)
-    g_ring.step(2)
-    v_far.step(2)
-    k_far.step(2)
-    v_own.step(3)
-    k_own.step(3)
-    turn(tiles // 2, 3 * tiles // 4)
-    v_far.step(3)
-    k_far.step(3)
+    v_far.second()
     v_own.step(4)
+    k_far.second()
     k_own.step(4)
-    turn(3 * tiles // 4, tiles)
-    v_far.step(4)
-    k_far.step(4)
-    rings = (v_own, k_own, v_far, k_far, q_ring, g_ring)
-    for ring in rings:
-        ring.end()
+    turn(tiles // 2, tiles)
+    loads[6].wait()
+    rings = (v_own, k_own, v_far, k_far)
+    for r in rings:
+        r.end()
+    for copy in sideways:
+        copy.wait_recv()
     total = jnp.zeros((16, ROWS), F32)
     for z in range(NZ):
         for j in range(NY):
             total = total + vals[z, j, ROWS : ROWS + 16, :].astype(F32)
     for j in range(NX):
         total = total + gs[j, ROWS : ROWS + 16, 0:HD].astype(F32)
-    places[...] = total[0:8].astype(jnp.int32)
+    seats = lax.broadcasted_iota(jnp.int32, (8, ROWS), 1)
+    lengths = jnp.zeros((8, ROWS), jnp.int32)
+    for d in range(4):
+        lengths = lengths + jnp.where(seats == d, docs[d], 0)
+    rows = lax.broadcasted_iota(jnp.int32, (8, ROWS), 0)
+    places[...] = jnp.where(rows == 1, lengths, total[0:8].astype(jnp.int32))
     z_v.wait_send()
     z_k.wait_send()
-    for ring in rings:
-        ring.drain()
-
-
-def live_keys(places, doc_lens, listed, query):
+    for r in rings:
+        r.drain()
+    for copy in sideways:
+        copy.wait_send()
+
+
+def live_keys(places, listed, query):
     starts = [jnp.int32(0)]
     for d in range(3):
-        starts.append(starts[-1] + doc_lens[d])
+        starts.append(starts[-1] + places[1, d])
     mine = places[0, KEY_BLOCKS + query]
     first_row = mine * BLK
     start = jnp.int32(0)
@@ -289,9 +341,9 @@
     )
 
 
-def stats_kernel(places, doc_lens, keys, vals, qs, gs, out, kept, listed):
+def stats_kernel(places, keys, vals, qs, gs, out, kept, listed):
     def visit(query, carry):
-        count, row, opens = live_keys(places, doc_lens, listed, query)
+        count, row, opens = live_keys(places, listed, query)
         q, g = head_stack(qs, query), head_stack(gs, query)
 
         def chunk_step(chunk, state):
@@ -348,13 +400,13 @@
 
 
 def back_kernel(
-    places, doc_lens, stats, keys, vals, qs, gs, dq, dk, dv, dk_sum, dv_sum, listed
+    places, stats, keys, vals, qs, gs, dq, dk, dv, dk_sum, dv_sum, listed
 ):
     dk_sum[...] = jnp.zeros_like(dk_sum)
     dv_sum[...] = jnp.zeros_like(dv_sum)
 
     def visit(query, carry):
-        count, row, opens = live_keys(places, doc_lens, listed, query)
+        count, row, opens = live_keys(places, listed, query)
         q, g = head_stack(qs, query), head_stack(gs, query)
         top, scale, delta = [stats[i, pl.ds(query, 1), :] for i in range(3)]
 
@@ -385,80 +437,105 @@
     dv[...] = dv_sum[...].astype(BF16)
 
 
+class Fold:
+    def __init__(self, block, me, n, ups, downs, got_far, got_half, got_near, made, got_last, sems):
+        self.block, self.me, self.n, self.peers, self.sems = block, me, n, (ups, downs), sems
+        self.got_far, self.got_half, self.got_near = got_far, got_half, got_near
+        self.made, self.got_last = made, got_last
+
+    def at(self, way, far):
+        return self.block(rem(self.me + (far if way == 0 else self.n - far), self.n))
+
+    def first(self):
+        self.far, self.half, self.near = [], [], []
+        for way, peers in enumerate(self.peers):
+            src = self.at(way, 4).at[way]
+            self.half.append(send(src, self.got_half.at[way], self.sems, way, peers[1]))
+            self.far.append(send(self.at(way, 3), self.got_far.at[way], self.sems, 2 + way, peers[0]))
+        for way, peers in enumerate(self.peers):
+            self.near.append(send(self.at(way, 1), self.got_near.at[way], self.sems, 4 + way, peers[0]))
+
+    def second(self):
+        self.last = []
+        for way, peers in enumerate(self.peers):
+            self.far[way].wait_recv()
+            self.half[way].wait_recv()
+            own, far, out = self.at(way, 2), self.got_far.at[way], self.made.at[way]
+            out[1 - way] = (own[1 - way].astype(F32) + far[1 - way].astype(F32)).astype(BF16)
+            out[way] = (
+                own[way].astype(F32) + far[way].astype(F32) + self.got_half[way].astype(F32)
+            ).astype(BF16)
+            self.last.append(send(out, self.got_last.at[way], self.sems, 6 + way, peers[1]))
+
+    def end(self):
+        for copy in self.near + self.last:
+            copy.wait_recv()
+
+    def total(self, z):
+        out = self.block(self.me)[z].astype(F32)
+        for way in range(2):
+            out = out + self.got_near[way, z].astype(F32) + self.got_last[way, z].astype(F32)
+        return out
+
+    def drain(self):
+        for copy in self.far + self.half + self.near + self.last:
+            copy.wait_send()
+
+
 def reduce_kernel(
     nl, dq, dk, dv, turned, w_key, d_query, d_value, d_input, d_wkey,
-    kv_got, kv_made, q_got, q_made, w_got, w_made, z_out, z_got, kg, kg_pair, xg, x_hop, w_own, w_pair,
-    w_part, in_part, in_got, zw_out, zw_got,
-    y_send, y_recv, x_send, x_recv, z_send, z_recv, s_send, s_recv, load_sem,
+    k_far, k_half, k_near, k_made, k_last, v_got, v_made, q_got, w_got, z_out, z_got,
+    kg, kg_pair, xg, w_own, w_pair, w_part, in_part, in_got, zw_out, zw_got,
+    k_send, k_recv, v_send, v_recv, w_send, w_recv, x_send, x_recv, z_send, z_recv, s_send, s_recv, load_sem,
 ):
     y, zh, x, t = place()
     zl, core = lax.div(t, jnp.int32(NC)), rem(t, NC)
-    up, down = device(rem(y + 1, NY), zh, x, t), device(rem(y + NY - 1, NY), zh, x, t)
+    others_y = [device(rem(y + j, NY), zh, x, t) for j in range(1, NY)]
+    ups, downs = others_y[:2], [others_y[-1], others_y[-2]]
     others_x = [device(y, zh, rem(x + j, NX), t) for j in range(1, NX)]
-    right, left = others_x[0], others_x[-1]
     partner = device(y, 1 - zh, x, t)
     sibling = device(y, zh, x, zl * NC + 1 - core)
     others_l = [device(y, zh, x, rem(zl + j, nl) * NC + core) for j in range(1, nl)]
-    x_sems, y_sems = (x_send, x_recv), (y_send, y_recv)
-    z_sems, s_sems = (z_send, z_recv), (s_send, s_recv)
+    x_sems, z_sems, s_sems = (x_send, x_recv), (z_send, z_recv), (s_send, s_recv)
 
     own_x = pltpu.make_async_copy(turned.at[x], xg.at[x], load_sem.at[0])
     own_w = pltpu.make_async_copy(w_key.at[:, core], w_own, load_sem.at[1])
     own_x.start()
     own_w.start()
-    meet([up, down, partner, sibling] + others_x + others_l)
-
-    def ring(arr, z, j):
-        return Reduce(
-            lambda o: arr.at[z, o], ROWS, y, NY, up, down,
-            (kv_got.at[j, 0], kv_got.at[j, 1]), (kv_made.at[j, 0], kv_made.at[j, 1]),
-            y_sems, 2 * HY * j,
-        )
-
-    k_far, v_far = ring(dk, 1 - zh, 0), ring(dv, 1 - zh, 1)
-    k_own, v_own = ring(dk, zh, 2), ring(dv, zh, 3)
-    rings = (k_far, k_own, v_far, v_own)
-    for r in rings:
-        r.step(1)
-    pairs = NZ * NY
-    opposite = rem(x + 2, NX)
-    x_next = send(turned.at[rem(x + 1, NX)], xg.at[x], x_sems, 0, right)
-    x_prev = send(turned.at[rem(x + NX - 1, NX)], xg.at[x], x_sems, 1, left)
-    lower, upper = pl.ds(0, pairs // 2), pl.ds(pairs // 2, pairs // 2)
-    hop_right = send(turned.at[opposite, lower], x_hop.at[0], x_sems, 2, right)
-    hop_left = send(turned.at[opposite, upper], x_hop.at[1], x_sems, 3, left)
+    meet(others_y + others_x + others_l + [partner, sibling])
+
+    fold = Fold(
+        lambda o: dk.at[:, o], y, NY, ups, downs, k_far, k_half, k_near, k_made, k_last, (k_send, k_recv)
+    )
+    fold.first()
+    x_sends = [
+        send(turned.at[rem(x + j, NX)], xg.at[x], x_sems, j - 1, others_x[j - 1]) for j in (2, 1, 3)
+    ]
     w_swap = send(w_key.at[:, 1 - core], w_pair, s_sems, 0, sibling)
-    q_ring = Reduce(
-        lambda o: dq.at[o], ROWS, x, NX, right, left,
-        (q_got.at[0], q_got.at[1]), (q_made.at[0], q_made.at[1]), x_sems, 4,
+    v_ring = Reduce(
+        lambda o: dv.at[:, o], NZ, y, NY, ups[0], downs[0],
+        (v_got.at[0], v_got.at[1]), (v_made.at[0], v_made.at[1]), (v_send, v_recv), 0,
     )
-    q_ring.step(1)
-    for r in rings:
-        r.step(2)
-    hop_right.wait_recv()
-    far_right = send(x_hop.at[0], xg.at[rem(x + NX - 1, NX), lower], x_sems, 8, right)
-    hop_left.wait_recv()
-    far_left = send(x_hop.at[1], xg.at[rem(x + 1, NX), upper], x_sems, 9, left)
-    for r in rings:
-        r.step(3)
-    q_ring.step(2)
-    for r in rings:
-        r.step(4)
-    z_out[0] = k_far.total().astype(BF16)
+    fold.second()
+    v_ring.step(1)
+    fold.end()
+    z_out[0] = fold.total(1 - zh).astype(BF16)
     z_key = send(z_out.at[0], z_got.at[0], z_sems, 0, partner)
-    key_sum = k_own.total()
-    z_out[1] = v_far.total().astype(BF16)
-    z_val = send(z_out.at[1], z_got.at[1], z_sems, 1, partner)
+    v_ring.step(2)
+    key_sum = fold.total(zh)
+    v_ring.step(3)
     z_key.wait_recv()
     kg[x] = (key_sum + z_got[0].astype(F32)).astype(BF16)
 
     kg_swap = send(kg.at[x], kg_pair, s_sems, 1, sibling)
-    kg_sends = [send(kg.at[x], kg.at[x], x_sems, 9 + j, others_x[j - 1]) for j in range(1, NX)]
+    kg_sends = [send(kg.at[x], kg.at[x], x_sems, 2 + j, others_x[j - 1]) for j in (2, 1, 3)]
+    q_sends = [
+        send(dq.at[rem(x + j, NX)], q_got.at[j - 1], x_sems, 5 + j, others_x[j - 1]) for j in (2, 1, 3)
+    ]
 
     own_w.wait()
     w_swap.wait_recv()
     kg_swap.wait_recv()
-    in_sends = []
     mine, pair = kg[x], kg_pair[...]
 
     def in_block(owner):
@@ -466,49 +543,61 @@
             mine, w_own[owner], NT, preferred_element_type=F32
         ) + lax.dot_general(pair, w_pair[owner], NT, preferred_element_type=F32)
 
-    for j in range(1, nl):
+    in_sends = []
+    for j in (2, 1, 3):
         in_part[j - 1] = in_block(rem(zl + j, nl)).astype(BF16)
         in_sends.append(send(in_part.at[j - 1], in_got.at[j - 1], s_sems, 1 + j, others_l[j - 1]))
+    v_ring.step(4)
 
     own_x.wait()
-    x_next.wait_recv()
-    x_prev.wait_recv()
-    far_right.wait_recv()
-    far_left.wait_recv()
-    for copy in kg_sends:
+    for copy in x_sends + kg_sends:
         copy.wait_recv()
-    product = jnp.zeros((pairs * BLK, HD), F32)
-    for src in range(NX):
-        block = xg[src].reshape(pairs * BLK, ROWS)
-        product = product + jnp.dot(block, kg[src], preferred_element_type=F32)
-    w_part[...] = product.astype(BF16).reshape(NY, NZ * BLK, HD)
-    w_ring = Reduce(
-        lambda o: w_part.at[o], NZ * BLK, y, NY, up, down,
-        (w_got.at[0], w_got.at[1]), (w_made.at[0], w_made.at[1]), y_sems, 8 * HY,
-    )
-    w_ring.step(1)
-    z_val.wait_recv()
-    d_value[...] = (v_own.total() + z_got[1].astype(F32)).astype(BF16)
-    w_ring.step(2)
-    d_query[...] = q_ring.total().astype(BF16)
-    w_ring.step(3)
+    heads = [kg[src] for src in range(NX)]
+
+    def w_block(owner):
+        out = jnp.zeros((NZ * BLK, HD), F32)
+        for src in range(NX):
+            rows = xg[src, pl.ds(owner * NZ, NZ)].reshape(NZ * BLK, ROWS)
+            out = out + jnp.dot(rows, heads[src], preferred_element_type=F32)
+        return out
+
+    w_sends = []
+    for j in (4, 3, 5, 2, 6, 1, 7):
+        w_part[j - 1] = w_block(rem(y + j, NY)).astype(BF16)
+        w_sends.append(send(w_part.at[j - 1], w_got.at[j - 1], (w_send, w_recv), j - 1, others_y[j - 1]))
+    zw_out[...] = w_block(y)
+    v_ring.end()
+    z_out[1] = v_ring.total(1 - zh).astype(BF16)
+    z_val = send(z_out.at[1], z_got.at[1], z_sems, 1, partner)
     in_sum = in_block(zl)
-    w_ring.step(4)
-    zw_out[...] = w_ring.total()
+    for copy in w_sends:
+        copy.wait_recv()
+    w_sum = zw_out[...]
+    for j in range(NY - 1):
+        w_sum = w_sum + w_got[j].astype(F32)
+    zw_out[...] = w_sum
     z_w = send(
         zw_out.at[pl.ds(pl.multiple_of((1 - zh) * BLK, BLK), BLK)], zw_got, z_sems, 2, partner
     )
-    for j, copy in enumerate(in_sends):
+    q_sum = dq[x].astype(F32)
+    for j, copy in enumerate(q_sends):
         copy.wait_recv()
+    for j in range(NX - 1):
+        q_sum = q_sum + q_got[j].astype(F32)
+    d_query[...] = q_sum.astype(BF16)
+    for copy in in_sends:
+        copy.wait_recv()
+    for j in range(nl - 1):
         in_sum = in_sum + in_got[j].astype(F32)
     d_input[...] = in_sum.astype(BF16)
+    z_val.wait_recv()
+    d_value[...] = (v_ring.total(zh) + z_got[1].astype(F32)).astype(BF16)
     z_w.wait_recv()
     d_wkey[...] = zw_out[pl.ds(pl.multiple_of(zh * BLK, BLK), BLK), :] + zw_got[...]
 
-    for r in rings + (q_ring, w_ring):
-        r.drain()
-    last = [x_next, x_prev, hop_right, hop_left, far_right, far_left, w_swap, z_key, z_val, kg_swap, z_w]
-    for copy in last + kg_sends + in_sends:
+    fold.drain()
+    v_ring.drain()
+    for copy in [w_swap, z_key, z_val, kg_swap, z_w] + x_sends + kg_sends + q_sends + in_sends + w_sends:
         copy.wait_send()
 
 
@@ -522,6 +611,21 @@
         has_side_effects=collective_id is not None,
         vmem_limit_bytes=VMEM_LIMIT,
     )
+
+
+def in_hbm(array):
+    return pltpu.with_memory_space_constraint(array, pltpu.HBM)
+
+
+def hand_over_kernel(*refs):
+    n = (len(refs) - 1) // 2
+    copies = [
+        pltpu.make_async_copy(refs[i], refs[n + i], refs[-1].at[i]) for i in range(n)
+    ]
+    for copy in copies:
+        copy.start()
+    for copy in copies:
+        copy.wait()
 
 
 def on_device(nl, inputs, w_key, values, queries, d_out, doc_lens, block_pos):
@@ -538,22 +642,24 @@
             shape((NX, pairs, BLK, ROWS), BF16),
             shape((8, ROWS), jnp.int32),
         ),
-        in_specs=[anywhere, anywhere, vmem, vmem, vmem, smem],
+        in_specs=[hbm] * 7,
         out_specs=(vmem,) * 6,
         scratch_shapes=[
             pltpu.VMEM((ROWS, width), BF16),
             pltpu.VMEM((width, HD), BF16),
-            dma(8 * HY), dma(8 * HY), dma(4 * HX), dma(4 * HX), dma(2), dma(2), dma(2),
+            pltpu.SMEM((4,), jnp.int32),
+            pltpu.SMEM((2,), jnp.int32),
+            dma(32), dma(32), dma(6), dma(6), dma(2), dma(2), dma(7),
         ],
         compiler_params=params(1),
         name="gather_rows",
-    )(inputs, w_key, values, queries, d_out, block_pos)
+    )(*(in_hbm(a) for a in (inputs, w_key, values, queries, d_out, doc_lens, block_pos)))
     keys = keys.reshape(KEY_BLOCKS * BLK, HD)
     vals = vals.reshape(pairs, ROWS + 16, HD)
     stats = pl.pallas_call(
         stats_kernel,
         out_shape=shape((3, QUERY_BLOCKS, STACK), F32),
-        in_specs=[smem, smem, vmem, vmem, vmem, vmem],
+        in_specs=[smem, vmem, vmem, vmem, vmem],
         out_specs=vmem,
         scratch_shapes=[
             pltpu.VMEM((QUERY_BLOCKS, 8, STACK), F32),
@@ -561,7 +667,7 @@
         ],
         compiler_params=params(),
         name="row_stats",
-    )(places, doc_lens, keys, vals, qs, gs)
+    )(places, keys, vals, qs, gs)
     stats = pl.pallas_call(
         share_kernel,
         out_shape=shape((3, QUERY_BLOCKS, STACK), F32),
@@ -580,7 +686,7 @@
             shape((KEY_BLOCKS * BLK, HD), BF16),
             shape((KEY_BLOCKS * BLK, HD), BF16),
         ),
-        in_specs=[smem, smem, vmem, vmem, vmem, vmem, vmem],
+        in_specs=[smem, vmem, vmem, vmem, vmem, vmem],
         out_specs=(vmem,) * 3,
         scratch_shapes=[
             pltpu.VMEM((KEY_BLOCKS * BLK, HD), F32),
@@ -589,11 +695,11 @@
         ],
         compiler_params=params(),
         name="back_tiles",
-    )(places, doc_lens, stats, keys, vals, qs, gs)
+    )(places, stats, keys, vals, qs, gs)
     slice_width = width // (nl * NC)
     w_split = w_key.reshape(nl, NC, slice_width, HD)
     block = (ROWS, HD)
-    return pl.pallas_call(
+    results = pl.pallas_call(
         functools.partial(reduce_kernel, nl),
         out_shape=(
             shape((ROWS, GROUP * HD), BF16),
@@ -601,33 +707,45 @@
             shape((ROWS, slice_width), BF16),
             shape((BLK, HD), F32),
         ),
-        in_specs=[vmem, vmem, vmem, anywhere, anywhere],
+        in_specs=[vmem, vmem, vmem, vmem, hbm],
         out_specs=(vmem,) * 4,
         scratch_shapes=[
-            pltpu.VMEM((4, 2, HY) + block, BF16),
-            pltpu.VMEM((4, 2, HY) + block, BF16),
-            pltpu.VMEM((2, HX, ROWS, GROUP * HD), BF16),
-            pltpu.VMEM((2, HX, ROWS, GROUP * HD), BF16),
-            pltpu.VMEM((2, HY) + block, BF16),
-            pltpu.VMEM((2, HY) + block, BF16),
+            pltpu.VMEM((2, NZ) + block, BF16),
+            pltpu.VMEM((2,) + block, BF16),
+            pltpu.VMEM((2, NZ) + block, BF16),
+            pltpu.VMEM((2, NZ) + block, BF16),
+            pltpu.VMEM((2, NZ) + block, BF16),
+            pltpu.VMEM((2, HY, NZ) + block, BF16),
+            pltpu.VMEM((2, HY, NZ) + block, BF16),
+            pltpu.VMEM((NX - 1, ROWS, GROUP * HD), BF16),
+            pltpu.VMEM((NY - 1,) + block, BF16),
             pltpu.VMEM((2,) + block, BF16),
             pltpu.VMEM((2,) + block, BF16),
             pltpu.VMEM((NX,) + block, BF16),
             pltpu.VMEM(block, BF16),
             pltpu.VMEM((NX, pairs, BLK, ROWS), BF16),
-            pltpu.VMEM((2, pairs // 2, BLK, ROWS), BF16),
             pltpu.VMEM((nl, slice_width, HD), BF16),
             pltpu.VMEM((nl, slice_width, HD), BF16),
-            pltpu.VMEM((NY,) + block, BF16),
+            pltpu.VMEM((NY - 1,) + block, BF16),
             pltpu.VMEM((nl - 1, ROWS, slice_width), BF16),
             pltpu.VMEM((nl - 1, ROWS, slice_width), BF16),
             pltpu.VMEM(block, F32),
             pltpu.VMEM((BLK, HD), F32),
-            dma(10 * HY), dma(10 * HY), dma(13), dma(13), dma(3), dma(3), dma(1 + nl), dma(1 + nl), dma(2),
+            dma(8), dma(8), dma(2 * HY), dma(2 * HY), dma(NY - 1), dma(NY - 1), dma(9), dma(9), dma(3), dma(3),
+            dma(1 + nl), dma(1 + nl), dma(2),
         ],
         compiler_params=params(3),
         name="reduce_grads",
-    )(dq, dk.reshape(NZ, NY, ROWS, HD), dv.reshape(NZ, NY, ROWS, HD), turned, w_split)
+    )(dq, dk.reshape(NZ, NY, ROWS, HD), dv.reshape(NZ, NY, ROWS, HD), turned, in_hbm(w_split))
+    return pl.pallas_call(
+        hand_over_kernel,
+        out_shape=tuple(shape(r.shape, r.dtype) for r in results),
+        in_specs=[vmem] * 4,
+        out_specs=(hbm,) * 4,
+        scratch_shapes=[dma(4)],
+        compiler_params=params(),
+        name="hand_over",
+    )(*results)
 
 
 def solution(mesh):

time: 121 us -> 97.7 us (0.81)
  the two profiles are of different devices: /device:TPU:8 before, /device:TPU:2 now
where the time goes in v2:
time: 97.7 us; the launch traced here: 97.5 us
  Pallas kernels  96.8 us (99%)
    pallas_call x1, Pallas kernels, on_device(): pl.pallas_call(functools.partial(reduce_kernel, nl), out_shape=(shape((RO...  40.7 us
    pallas_call x1, Pallas kernels, on_device(): pl.pallas_call(gather_kernel, out_shape=(shape((NZ, NY, ROWS, HD), BF16),...  30.5 us
    pallas_call x1, Pallas kernels, on_device(): pl.pallas_call(back_kernel, out_shape=(shape((NX, ROWS, GROUP * HD), BF16...  10.4 us
    pallas_call x1, Pallas kernels, on_device(): pl.pallas_call(share_kernel, out_shape=shape((3, QUERY_BLOCKS, STACK), F3...  7.66 us
    pallas_call x1, Pallas kernels, on_device(): pl.pallas_call(stats_kernel, out_shape=shape((3, QUERY_BLOCKS, STACK), F3...  6.88 us

profile of v2, /device:TPU:2, one launch (start us, length us, event | category | flops | bytes accessed | tf_op | source)
XLA Modules:
  0.0 97.5 jit_solution(16323171466484968167)
XLA Ops:
  0.6 30.5 %gather_rows.1 = (bf16[2,8,128,128]{3,2,1,0:T(8,128)(2,1)S(1)}, bf16[2,8,144,128]{3,2,1,0:T(8,128)(2,1)S(1)}, bf16[4,128,512]{2,1,0:T(8,128)(2,1)S(1)}, bf16[4,1...) custom-call(bf16[128,4096]{1,0:T(8,128)(2,1)} %inputs.1, ...), custom_call_target="tpu_custom_call" | custom-call | tf_op jit(solution)/shard_map/gather_rows/pallas_call | solution.py:635
  31.1 6.9 %row_stats.1.stats = f32[3,8,256]{2,1,0:T(8,128)S(1)} custom-call(s32[8,128]{1,0:T(8,128)S(1)} %get-tuple-element.17.places, bf16[2048,128]{1,0:T(8,128)(2,1)S(1)} %bitcast.7, bf16[16,144,128]{2,1,0:T(8,128)(2,1)S(1)} %bitcast.5, bf16[4,128,512]{2,1,0:T(8,128)(2,1)S(1)} %get-tuple-element.20.qs, bf16[4,144,512]{2,1,0:T(8,128)(2,1)S(1)} %get-tuple-element.21.gs), custom_call_target="tpu_custom_call" | custom-call | tf_op jit(solution)/shard_map/row_stats/pallas_call | solution.py:659
  38.0 7.7 %share_stats.1.stats = f32[3,8,256]{2,1,0:T(8,128)S(1)} custom-call(f32[3,8,256]{2,1,0:T(8,128)S(1)} %row_stats.1.stats), custom_call_target="tpu_custom_call" | custom-call | tf_op jit(solution)/shard_map/share_stats/pallas_call | solution.py:671
  45.7 10.4 %back_tiles.1 = (bf16[4,128,512]{2,1,0:T(8,128)(2,1)S(1)}, bf16[2048,128]{1,0:T(8,128)(2,1)S(1)}, bf16[2048,128]{1,0:T(8,128)(2,1)S(1)}) custom-call(s32[8,128]{1,0:T(8,128)S(1)} %get-tuple-element.17.places, f32[3,8,256]{2,1,0:T(8,128)S(1)} %share_stats.1.stats, bf16[2048,128]{1,0:T(8,128)(2,1)S(1)} %bitcast.8, bf16[16,144,128]{2,1,0:T(8,128)(2,1)S(1)} %bitcast.6, ...), custom_call_target="tpu_custom_call" | custom-call | tf_op jit(solution)/shard_map/back_tiles/pallas_call | solution.py:682
  56.1 40.7 %reduce_grads.1 = (bf16[128,512]{1,0:T(8,128)(2,1)S(1)}, bf16[128,128]{1,0:T(8,128)(2,1)S(1)}, bf16[128,512]{1,0:T(8,128)(2,1)S(1)}, f32[64,128]{1,0:T(8,128)S(1)}) custom-call(bf16[4,128,512]{2,1,0:T(8,128)(2,1)S(1)} %get-tuple-element.22.dq, bf16[2,8,128,128]{3,2,1,0:T(8,128)(2,1)S(1)} %bitcast.9, bf16[2,8,128,128]{3,2,1,0:T(8,128)(2,1)S(1)} %bitcast.10, ...), custom_call_target="tpu_custom_call" | custom-call | tf_op jit(solution)/shard_map/reduce_grads/pallas_call | solution.py:702
  96.7 0.7 hand_over.1

commit v3 on v2

v3 whole, which is shorter than its diff:
```python
import functools
import math

import jax
import jax.numpy as jnp
from jax import lax
from jax.experimental import pallas as pl
from jax.experimental.pallas import tpu as pltpu
from jax.sharding import PartitionSpec as P

MESH = pl.DeviceIdType.MESH
F32, BF16 = jnp.float32, jnp.bfloat16
HD, BLK, GROUP, ROWS = 128, 64, 4, 128
NX, NZ, NY, NC = 4, 2, 8, 2
HY, HX = NY // 2, NX // 2
KEY_BLOCKS = 2 * NZ * NY
QUERY_BLOCKS = 2 * NX
STACK = GROUP * BLK
CHUNK = 4
CHUNKS = KEY_BLOCKS // CHUNK
SIDE = 2
PARTS = 4
LIST, COUNTS, ITEMS, TOTAL, PLAN = 40, 320, 336, 416, 512
SCALE = 1.0 / math.sqrt(HD)
LOG2 = SCALE / math.log(2.0)
LOW = -1e30
FLOOR = -1e29
NT = (((1,), (1,)), ((), ()))
VMEM_LIMIT = 40 * 1024 * 1024

vmem = pl.BlockSpec(memory_space=pltpu.VMEM)
smem = pl.BlockSpec(memory_space=pltpu.SMEM)
hbm = pl.BlockSpec(memory_space=pltpu.HBM)


def rem(a, n):
    return lax.rem(a, jnp.int32(n))


def place():
    dp, tensor = lax.axis_index("dp"), lax.axis_index("tensor")
    x = rem(dp, NX)
    rest = lax.div(dp, jnp.int32(NX))
    return lax.div(rest, jnp.int32(NZ)), rem(rest, NZ), x, tensor


def device(y, zh, x, tensor):
    return ((y * NZ + zh) * NX + x, tensor)


def greet(peers):
    barrier = pltpu.get_barrier_semaphore()
    for peer in peers:
        pl.semaphore_signal(barrier, inc=1, device_id=peer, device_id_type=MESH)


def meet(peers):
    pl.semaphore_wait(pltpu.get_barrier_semaphore(), len(peers))


def send(src, dst, sems, index, peer):
    copy = pltpu.make_async_remote_copy(
        src_ref=src,
        dst_ref=dst,
        send_sem=sems[0].at[index],
        recv_sem=sems[1].at[index],
        device_id=peer,
        device_id_type=MESH,
    )
    copy.start()
    return copy


class Tree:
    def __init__(self, block, half, me, n, ups, downs, sems, base):
        self.block, self.half, self.me, self.n = block, half, me, n
        self.ups, self.downs, self.sems, self.base = ups, downs, sems, base

    def first(self):
        own = self.block(self.me)
        self.near = [
            send(own, own, self.sems, self.base + i, peer)
            for i, peer in enumerate((self.ups[1], self.downs[1], self.ups[0], self.downs[0]))
        ]

    def second(self):
        self.far = []
        for way, peers in enumerate((self.ups, self.downs)):
            self.near[way].wait_recv()
            ref = self.block(rem(self.me + (self.n - 2 if way == 0 else 2), self.n))
            half = self.half(ref, way)
            self.far.append(send(half, half, self.sems, self.base + 4 + 2 * way, peers[1]))
            self.far.append(send(ref, ref, self.sems, self.base + 5 + 2 * way, peers[0]))

    def end(self):
        for copy in self.near[2:] + self.far:
            copy.wait_recv()

    def drain(self):
        for copy in self.near + self.far:
            copy.wait_send()


def gather_kernel(
    inputs, w_key, values, queries, d_out, doc_lens, block_pos, keys, vals, qs, gs, turned, places,
    x_buf, w_buf, docs, pos, y_send, y_recv, x_send, x_recv, z_send, z_recv, load_sem,
):
    y, zh, x, t = place()
    ups = [device(rem(y + j, NY), zh, x, t) for j in (1, 2)]
    downs = [device(rem(y + NY - j, NY), zh, x, t) for j in (1, 2)]
    others_x = [device(y, zh, rem(x + j, NX), t) for j in range(1, NX)]
    partner = device(y, 1 - zh, x, t)
    peers = [partner] + ups + downs + others_x
    greet(peers)
    loads = [
        pltpu.make_async_copy(src, dst, load_sem.at[i])
        for i, (src, dst) in enumerate(
            (
                (block_pos, pos),
                (values, vals.at[zh, y, pl.ds(0, ROWS)]),
                (d_out, gs.at[x, pl.ds(0, ROWS)]),
                (queries, qs.at[x]),
                (doc_lens, docs),
            )
        )
    ]
    depth = inputs.shape[1] // PARTS
    parts = []
    for i in range(PARTS):
        cut = slice(i * depth, (i + 1) * depth)
        parts.append((
            pltpu.make_async_copy(w_key.at[cut], w_buf.at[cut], load_sem.at[5 + 2 * i]),
            pltpu.make_async_copy(inputs.at[:, cut], x_buf.at[:, cut], load_sem.at[6 + 2 * i]),
        ))
    for load in loads + [load for pair in parts for load in pair]:
        load.start()
    loads[0].wait()
    lane = lax.broadcasted_iota(jnp.int32, (16, ROWS), 1)
    first = 2 * (zh * NY + y)
    mine = jnp.where(lane == first, pos[0], 0) + jnp.where(lane == first + 1, pos[1], 0)
    seat = KEY_BLOCKS + 2 * x
    here = jnp.where(lane == seat, pos[0], 0) + jnp.where(lane == seat + 1, pos[1], 0)
    vals[zh, y, ROWS : ROWS + 16, :] = mine.astype(F32).astype(BF16)
    gs[x, ROWS : ROWS + 16, 0:HD] = here.astype(F32).astype(BF16)
    gs[x, ROWS : ROWS + 16, HD:] = jnp.zeros((16, (GROUP - 1) * HD), BF16)
    loads[1].wait()
    meet(peers)

    y_sems, x_sems, z_sems = (y_send, y_recv), (x_send, x_recv), (z_send, z_recv)

    def half_k(ref, way):
        return ref.at[pl.ds(way * 64, 64)]

    def half_v(ref, way):
        return ref.at[pl.ds(0, 64)] if way == 0 else ref.at[pl.ds(64, ROWS + 16 - 64)]

    def tree(arr, half, z, base):
        return Tree(lambda o: arr.at[z, o], half, y, NY, ups, downs, y_sems, base)

    v_own, k_own = tree(vals, half_v, zh, 0), tree(keys, half_k, zh, 8)
    v_far, k_far = tree(vals, half_v, 1 - zh, 16), tree(keys, half_k, 1 - zh, 24)

    z_v = send(vals.at[zh, y], vals.at[zh, y], z_sems, 0, partner)
    v_own.first()
    sideways = []
    loads[2].wait()
    for j in (2, 1, 3):
        sideways.append(send(gs.at[x], gs.at[x], x_sems, j - 1, others_x[j - 1]))
    loads[3].wait()
    for j in (2, 1, 3):
        sideways.append(send(qs.at[x], qs.at[x], x_sems, j + 2, others_x[j - 1]))
    projected = jnp.zeros((ROWS, HD), F32)
    for i, pair in enumerate(parts):
        cut = slice(i * depth, (i + 1) * depth)
        for load in pair:
            load.wait()
        projected = projected + jnp.dot(
            x_buf[:, cut], w_buf[cut, :], preferred_element_type=F32
        )
    keys[zh, y] = projected.astype(BF16)
    z_k = send(keys.at[zh, y], keys.at[zh, y], z_sems, 1, partner)
    k_own.first()

    def turn(first, last):
        def body(j, carry):
            tile = x_buf[:, pl.ds(pl.multiple_of(j * 128, 128), 128)].T
            for part in range(2):
                b = 2 * j + part
                pair = lax.div(b, jnp.int32(NX))
                turned[rem(b, NX), rem(pair, NZ), lax.div(pair, jnp.int32(NZ))] = tile[
                    part * 64 : part * 64 + 64
                ]
            return carry

        lax.fori_loop(first, last, body, 0)

    tiles = inputs.shape[1] // 128
    turn(0, tiles // 4)
    v_own.second()
    z_v.wait_recv()
    v_far.first()
    k_own.second()
    z_k.wait_recv()
    k_far.first()
    turn(tiles // 4, tiles // 2)
    v_far.second()
    k_far.second()
    turn(tiles // 2, tiles)
    loads[4].wait()
    rings = (v_own, k_own, v_far, k_far)
    for r in rings:
        r.end()
    for copy in sideways:
        copy.wait_recv()
    total = jnp.zeros((16, ROWS), F32)
    for z in range(NZ):
        for j in range(NY):
            total = total + vals[z, j, ROWS : ROWS + 16, :].astype(F32)
    for j in range(NX):
        total = total + gs[j, ROWS : ROWS + 16, 0:HD].astype(F32)
    seats = lax.broadcasted_iota(jnp.int32, (8, ROWS), 1)
    lengths = jnp.zeros((8, ROWS), jnp.int32)
    for d in range(4):
        lengths = lengths + jnp.where(seats == d, docs[d], 0)
    rows = lax.broadcasted_iota(jnp.int32, (8, ROWS), 0)
    places[...] = jnp.where(rows == 1, lengths, total[0:8].astype(jnp.int32))
    z_v.wait_send()
    z_k.wait_send()
    for r in rings:
        r.drain()
    for copy in sideways:
        copy.wait_send()


def doc_starts(places):
    starts = [jnp.int32(0)]
    for d in range(3):
        starts.append(starts[-1] + places[1, d])
    return starts


def make_plan(places, plan):
    starts = doc_starts(places)

    def visit(query, items):
        mine = places[0, KEY_BLOCKS + query]
        start = jnp.int32(0)
        for s in starts[1:]:
            start = jnp.where(s <= mine * BLK, s, start)
        low = lax.div(start, jnp.int32(BLK))
        begin = query * LIST
        count = jnp.int32(0)
        for b in range(KEY_BLOCKS):
            pk = places[0, b]
            plan[begin + count] = jnp.int32(b)
            count = count + ((pk <= mine) & (pk >= low)).astype(jnp.int32)
        for j in range(CHUNK):
            plan[begin + count + j] = jnp.int32(0)
        plan[COUNTS + query] = count
        for c in range(CHUNKS):
            plan[ITEMS + items] = query * 16 + c
            items = items + (count > c * CHUNK).astype(jnp.int32)
        return items

    items = lax.fori_loop(0, QUERY_BLOCKS, visit, jnp.int32(0))
    plan[ITEMS + items] = jnp.int32(0)
    plan[TOTAL] = items


def item_of(places, plan, starts, at):
    real = at < plan[TOTAL]
    code = plan[ITEMS + at]
    query, chunk = code >> 4, code & 15
    count = jnp.where(real, plan[COUNTS + query], 0)
    row = places[0, KEY_BLOCKS + query] * BLK + (
        lax.broadcasted_iota(jnp.int32, (1, 2 * BLK), 1) & (BLK - 1)
    )
    opens = jnp.zeros((1, 2 * BLK), jnp.int32)
    for s in starts[1:]:
        opens = jnp.where(s <= row, s, opens)
    return query, chunk, real, count, row, opens


def key_chunk(places, plan, item, keys, vals):
    query, chunk, _, count, row, opens = item
    iota = lax.broadcasted_iota(jnp.int32, (BLK, 2 * BLK), 0)
    ks, vs, terms, blocks = [], [], [], []
    for j in range(CHUNK):
        at = chunk * CHUNK + j
        b = plan[query * LIST + at]
        base = jnp.where(at < count, places[0, b] * BLK, jnp.int32(1 << 20))
        ks.append(keys[pl.ds(pl.multiple_of(b * BLK, BLK), BLK), :])
        vs.append(vals[b >> 1, pl.ds(pl.multiple_of((b & 1) * BLK, BLK), BLK), :])
        ok = (iota >= opens - base) & (iota <= row - base)
        term = jnp.where(ok, 0.0, LOW)
        terms.append(jnp.concatenate([term, term], axis=1))
        blocks.append(b)
    return (
        jnp.concatenate(ks, axis=0),
        jnp.concatenate(vs, axis=0),
        jnp.concatenate(terms, axis=0),
        blocks,
    )


def head_stack(ref, query):
    rows = pl.ds(pl.multiple_of((query & 1) * BLK, BLK), BLK)
    return jnp.concatenate(
        [ref[query >> 1, rows, h * HD : (h + 1) * HD] for h in range(GROUP)], axis=0
    )


def stats_kernel(places, keys, vals, qs, gs, out, plan, kept):
    make_plan(places, plan)
    starts = doc_starts(places)
    for c in range(CHUNKS):
        kept[c, 0] = jnp.full((QUERY_BLOCKS, STACK), FLOOR, F32)
        kept[c, 1] = jnp.zeros((QUERY_BLOCKS, STACK), F32)
        kept[c, 2] = jnp.zeros((QUERY_BLOCKS, STACK), F32)

    def step(i, carry):
        found = []
        for part in range(SIDE):
            item = item_of(places, plan, starts, i * SIDE + part)
            k, v, term, _ = key_chunk(places, plan, item, keys, vals)
            q, g = head_stack(qs, item[0]), head_stack(gs, item[0])
            score = lax.dot_general(k, q, NT, preferred_element_type=F32) * LOG2 + term
            d_prob = lax.dot_general(v, g, NT, preferred_element_type=F32)
            top = jnp.maximum(FLOOR, jnp.max(score, axis=0, keepdims=True))
            e = jnp.exp2(score - top)
            found.append((
                item, top, jnp.sum(e, axis=0, keepdims=True), jnp.sum(e * d_prob, axis=0, keepdims=True)
            ))
        for item, top, mass, weighted in found:
            slot = jnp.where(item[2], item[1], CHUNKS)
            for j, value in enumerate((top, mass, weighted)):
                kept[slot, j, pl.ds(item[0], 1), :] = value
        return carry

    lax.fori_loop(0, lax.div(plan[TOTAL] + (SIDE - 1), jnp.int32(SIDE)), step, 0)
    top = kept[0, 0]
    for c in range(1, CHUNKS):
        top = jnp.maximum(top, kept[c, 0])
    mass, weighted = jnp.zeros_like(top), jnp.zeros_like(top)
    for c in range(CHUNKS):
        shrink = jnp.exp2(kept[c, 0] - top)
        mass = mass + kept[c, 1] * shrink
        weighted = weighted + kept[c, 2] * shrink
    out[0], out[1], out[2] = top, mass, weighted


def share_kernel(stats, out, got, send_sem, recv_sem):
    y, zh, x, t = place()
    peers = [device(y, zh, rem(x + j, NX), t) for j in range(1, NX)]
    greet(peers)
    meet(peers)
    copies = [send(stats, got.at[j], (send_sem, recv_sem), j, peer) for j, peer in enumerate(peers)]
    for copy in copies:
        copy.wait_recv()
    parts = [[stats[i] for i in range(3)]] + [[got[j, i] for i in range(3)] for j in range(NX - 1)]
    top = parts[0][0]
    for p in parts[1:]:
        top = jnp.maximum(top, p[0])
    mass = jnp.zeros_like(top)
    weighted = jnp.zeros_like(top)
    for p in parts:
        shrink = jnp.exp2(p[0] - top)
        mass = mass + p[1] * shrink
        weighted = weighted + p[2] * shrink
    out[0] = top
    out[1] = 1.0 / mass
    out[2] = weighted / mass
    for copy in copies:
        copy.wait_send()


def back_kernel(
    places, plan, stats, keys, vals, qs, gs, dq, dk, dv, dq_sum, dk_sum, dv_sum
):
    starts = doc_starts(places)
    dq_sum[...] = jnp.zeros_like(dq_sum)
    dk_sum[...] = jnp.zeros_like(dk_sum)
    dv_sum[...] = jnp.zeros_like(dv_sum)

    def step(i, carry):
        found = []
        for part in range(SIDE):
            item = item_of(places, plan, starts, i * SIDE + part)
            query = item[0]
            k, v, term, blocks = key_chunk(places, plan, item, keys, vals)
            q, g = head_stack(qs, query), head_stack(gs, query)
            top, scale, delta = [stats[j, pl.ds(query, 1), :] for j in range(3)]
            score = lax.dot_general(k, q, NT, preferred_element_type=F32) * LOG2 + term
            d_prob = lax.dot_general(v, g, NT, preferred_element_type=F32)
            prob = jnp.exp2(score - top) * scale
            d_score = (prob * (d_prob - delta)).astype(BF16)
            dv_part = jnp.dot(prob.astype(BF16), g, preferred_element_type=F32)
            dk_part = jnp.dot(d_score, q, preferred_element_type=F32)
            dq_part = jnp.dot(k.T, d_score, preferred_element_type=F32)
            found.append((query, blocks, dq_part, dk_part, dv_part))
        for query, blocks, dq_part, dk_part, dv_part in found:
            dq_sum[query] += dq_part
            for j, b in enumerate(blocks):
                rows = pl.ds(pl.multiple_of(b * BLK, BLK), BLK)
                dv_sum[rows, :] += dv_part[j * BLK : (j + 1) * BLK]
                dk_sum[rows, :] += dk_part[j * BLK : (j + 1) * BLK]
        return carry

    lax.fori_loop(0, lax.div(plan[TOTAL] + (SIDE - 1), jnp.int32(SIDE)), step, 0)
    for query in range(QUERY_BLOCKS):
        dq_rows = (dq_sum[query] * SCALE).T.astype(BF16)
        rows = slice((query % 2) * BLK, (query % 2 + 1) * BLK)
        for h in range(GROUP):
            dq[query // 2, rows, h * HD : (h + 1) * HD] = dq_rows[h * BLK : (h + 1) * BLK]
    dk[...] = (dk_sum[...] * SCALE).astype(BF16)
    dv[...] = dv_sum[...].astype(BF16)


class Fold:
    def __init__(self, block, me, n, ups, downs, far, near, made, last, sems, base):
        self.block, self.me, self.n, self.peers, self.sems, self.base = block, me, n, (ups, downs), sems, base
        self.got_far, self.got_near, self.made, self.got_last = far, near, made, last

    def at(self, way, far):
        return self.block(rem(self.me + (far if way == 0 else self.n - far), self.n))

    def go(self, src, dst, i, peer):
        return send(src, dst, self.sems, self.base + i, peer)

    def first(self):
        self.far, self.half, self.near = [], [], []
        for way, peers in enumerate(self.peers):
            part = pl.ds(way * (ROWS // 2), ROWS // 2)
            self.half.append(
                self.go(self.at(way, 4).at[part], self.got_far.at[way, pl.ds(ROWS, ROWS // 2)], way, peers[1])
            )
            self.far.append(
                self.go(self.at(way, 3), self.got_far.at[way, pl.ds(0, ROWS)], 2 + way, peers[0])
            )
        for way, peers in enumerate(self.peers):
            self.near.append(self.go(self.at(way, 1), self.got_near.at[way], 4 + way, peers[0]))

    def second(self):
        self.last = []
        middle = ROWS // 2
        for way, peers in enumerate(self.peers):
            self.far[way].wait_recv()
            self.half[way].wait_recv()
            own, far, out = self.at(way, 2), self.got_far.at[way], self.made.at[way]
            with_half = pl.ds(way * middle, middle)
            without = pl.ds((1 - way) * middle, middle)
            out[without] = (own[without].astype(F32) + far[without].astype(F32)).astype(BF16)
            out[with_half] = (
                own[with_half].astype(F32)
                + far[with_half].astype(F32)
                + far[pl.ds(ROWS, middle)].astype(F32)
            ).astype(BF16)
            self.last.append(self.go(out, self.got_last.at[way], 6 + way, peers[1]))

    def total(self):
        for copy in self.near + self.last:
            copy.wait_recv()
        out = self.block(self.me)[...].astype(F32)
        for way in range(2):
            out = out + self.got_near[way].astype(F32) + self.got_last[way].astype(F32)
        return out

    def drain(self):
        for copy in self.far + self.half + self.near + self.last:
            copy.wait_send()


def reduce_kernel(
    dq, dk, dv, turned, w_key, d_query, d_value, d_input, d_wkey,
    f_far, f_near, f_made, f_last, q_got, w_got, z_out, z_got,
    kg, kg_quad, xg, w_all, w_part, in_part, in_got, zw_out, zw_got,
    f_send, f_recv, w_send, w_recv, x_send, x_recv, z_send, z_recv, s_send, s_recv, load_sem,
):
    y, zh, x, t = place()
    zl, core = lax.div(t, jnp.int32(NC)), rem(t, NC)
    others_y = [device(rem(y + j, NY), zh, x, t) for j in range(1, NY)]
    ups, downs = others_y[:2], [others_y[-1], others_y[-2]]
    others_x = [device(y, zh, rem(x + j, NX), t) for j in range(1, NX)]
    partner = device(y, 1 - zh, x, t)
    half, quarter = lax.div(zl, jnp.int32(2)), rem(zl, 2)
    sibling = device(y, zh, x, zl * NC + 1 - core)
    across = [device(y, zh, x, (zl + 1 - 2 * quarter) * NC + c) for c in (core, 1 - core)]
    quad = [sibling] + across
    over = device(y, zh, x, rem(zl + 2, 4) * NC + core)
    x_sems, z_sems, s_sems = (x_send, x_recv), (z_send, z_recv), (s_send, s_recv)
    peers = [partner] + others_y + others_x + quad + [over]
    greet(peers)
    own_x = pltpu.make_async_copy(turned.at[x], xg.at[x], load_sem.at[0])
    own_w = pltpu.make_async_copy(w_key.at[:, quarter, core], w_all.at[0], load_sem.at[1])
    own_x.start()
    own_w.start()
    meet(peers)

    def fold(arr, z, i):
        return Fold(
            lambda o: arr.at[z, o], y, NY, ups, downs,
            f_far.at[i], f_near.at[i], f_made.at[i], f_last.at[i], (f_send, f_recv), 8 * i,
        )

    far = 1 - zh
    k_far, k_own = fold(dk, far, 0), fold(dk, zh, 1)
    v_far, v_own = fold(dv, far, 2), fold(dv, zh, 3)
    k_far.first()
    k_own.first()
    x_sends = [
        send(turned.at[rem(x + j, NX)], xg.at[x], x_sems, j - 1, others_x[j - 1]) for j in (2, 1, 3)
    ]
    w_sides = ((quarter, 1 - core), (1 - quarter, core), (1 - quarter, 1 - core))
    w_swaps = [
        send(w_key.at[:, q, c], w_all.at[j + 1], s_sems, j, quad[j]) for j, (q, c) in enumerate(w_sides)
    ]
    k_far.second()
    k_own.second()
    z_out[0] = k_far.total().astype(BF16)
    z_key = send(z_out.at[0], z_got.at[0], z_sems, 0, partner)
    v_far.first()
    v_own.first()
    key_sum = k_own.total()
    z_key.wait_recv()
    kg[x] = (key_sum + z_got[0].astype(F32)).astype(BF16)

    kg_sends = [send(kg.at[x], kg.at[x], x_sems, 2 + j, others_x[j - 1]) for j in (2, 1, 3)]
    kg_swaps = [send(kg.at[x], kg_quad.at[j], s_sems, 3 + j, quad[j]) for j in range(3)]
    q_sends = [
        send(dq.at[rem(x + j, NX)], q_got.at[j - 1], x_sems, 5 + j, others_x[j - 1]) for j in (2, 1, 3)
    ]
    v_far.second()
    v_own.second()
    own_w.wait()
    for copy in w_swaps + kg_swaps:
        copy.wait_recv()
    quad_heads = [kg[x]] + [kg_quad[j] for j in range(3)]

    def in_block(h):
        out = jnp.zeros((ROWS, w_all.shape[2]), F32)
        for j, head in enumerate(quad_heads):
            out = out + lax.dot_general(head, w_all[j, h], NT, preferred_element_type=F32)
        return out

    in_part[...] = in_block(1 - half).astype(BF16)
    in_send = send(in_part, in_got, s_sems, 6, over)

    own_x.wait()
    for copy in x_sends + kg_sends:
        copy.wait_recv()
    heads = [kg[src] for src in range(NX)]
    w_sends = []
    for turn, z in enumerate((far, zh)):
        product = jnp.zeros((NY * BLK, HD), F32)
        for src in range(NX):
            rows = xg[src, z].reshape(NY * BLK, ROWS)
            product = product + jnp.dot(rows, heads[src], preferred_element_type=F32)
        w_part[turn] = product.astype(BF16).reshape(NY, BLK, HD)
        for j in (4, 3, 5, 2, 6, 1, 7):
            w_sends.append(
                send(
                    w_part.at[turn, rem(y + j, NY)], w_got.at[turn, j - 1],
                    (w_send, w_recv), turn * (NY - 1) + j - 1, others_y[j - 1],
                )
            )

    def w_total(turn):
        for copy in w_sends[turn * (NY - 1) : (turn + 1) * (NY - 1)]:
            copy.wait_recv()
        out = w_part[turn, y].astype(F32)
        for j in range(NY - 1):
            out = out + w_got[turn, j].astype(F32)
        return out

    z_out[1] = v_far.total().astype(BF16)
    z_val = send(z_out.at[1], z_got.at[1], z_sems, 1, partner)
    in_sum = in_block(half)
    zw_out[...] = w_total(0)
    z_w = send(zw_out, zw_got, z_sems, 2, partner)
    q_sum = dq[x].astype(F32)
    for copy in q_sends:
        copy.wait_recv()
    for j in range(NX - 1):
        q_sum = q_sum + q_got[j].astype(F32)
    d_query[...] = q_sum.astype(BF16)
    in_send.wait_recv()
    d_input[...] = (in_sum + in_got[...].astype(F32)).astype(BF16)
    z_val.wait_recv()
    d_value[...] = (v_own.total() + z_got[1].astype(F32)).astype(BF16)
    w_sum = w_total(1)
    z_w.wait_recv()
    d_wkey[...] = w_sum + zw_got[...]

    for f in (k_far, k_own, v_far, v_own):
        f.drain()
    for copy in [z_key, z_val, z_w, in_send] + x_sends + kg_sends + q_sends + w_sends + w_swaps + kg_swaps:
        copy.wait_send()


def dma(n):
    return pltpu.SemaphoreType.DMA((n,))


def params(collective_id=None):
    return pltpu.CompilerParams(
        collective_id=collective_id,
        has_side_effects=collective_id is not None,
        vmem_limit_bytes=VMEM_LIMIT,
    )


def in_hbm(array):
    return pltpu.with_memory_space_constraint(array, pltpu.HBM)


def hand_over_kernel(*refs):
    n = (len(refs) - 1) // 2
    copies = [
        pltpu.make_async_copy(refs[i], refs[n + i], refs[-1].at[i]) for i in range(n)
    ]
    for copy in copies:
        copy.start()
    for copy in copies:
        copy.wait()


def on_device(nl, inputs, w_key, values, queries, d_out, doc_lens, block_pos):
    width = inputs.shape[1]
    pairs = NZ * NY
    shape = jax.ShapeDtypeStruct
    keys, vals, qs, gs, turned, places = pl.pallas_call(
        gather_kernel,
        out_shape=(
            shape((NZ, NY, ROWS, HD), BF16),
            shape((NZ, NY, ROWS + 16, HD), BF16),
            shape((NX, ROWS, GROUP * HD), BF16),
            shape((NX, ROWS + 16, GROUP * HD), BF16),
            shape((NX, NZ, NY, BLK, ROWS), BF16),
            shape((8, ROWS), jnp.int32),
        ),
        in_specs=[hbm] * 7,
        out_specs=(vmem,) * 6,
        scratch_shapes=[
            pltpu.VMEM((ROWS, width), BF16),
            pltpu.VMEM((width, HD), BF16),
            pltpu.SMEM((4,), jnp.int32),
            pltpu.SMEM((2,), jnp.int32),
            dma(32), dma(32), dma(6), dma(6), dma(2), dma(2), dma(5 + 2 * PARTS),
        ],
        compiler_params=params(1),
        name="gather_rows",
    )(*(in_hbm(a) for a in (inputs, w_key, values, queries, d_out, doc_lens, block_pos)))
    keys = keys.reshape(KEY_BLOCKS * BLK, HD)
    vals = vals.reshape(pairs, ROWS + 16, HD)
    stats, plan = pl.pallas_call(
        stats_kernel,
        out_shape=(shape((3, QUERY_BLOCKS, STACK), F32), shape((PLAN,), jnp.int32)),
        in_specs=[smem, vmem, vmem, vmem, vmem],
        out_specs=(vmem, smem),
        scratch_shapes=[pltpu.VMEM((CHUNKS + 1, 3, QUERY_BLOCKS, STACK), F32)],
        compiler_params=params(),
        name="row_stats",
    )(places, keys, vals, qs, gs)
    stats = pl.pallas_call(
        share_kernel,
        out_shape=shape((3, QUERY_BLOCKS, STACK), F32),
        in_specs=[vmem],
        out_specs=vmem,
        scratch_shapes=[
            pltpu.VMEM((NX - 1, 3, QUERY_BLOCKS, STACK), F32), dma(NX - 1), dma(NX - 1),
        ],
        compiler_params=params(2),
        name="share_stats",
    )(stats)
    dq, dk, dv = pl.pallas_call(
        back_kernel,
        out_shape=(
            shape((NX, ROWS, GROUP * HD), BF16),
            shape((KEY_BLOCKS * BLK, HD), BF16),
            shape((KEY_BLOCKS * BLK, HD), BF16),
        ),
        in_specs=[smem, smem, vmem, vmem, vmem, vmem, vmem],
        out_specs=(vmem,) * 3,
        scratch_shapes=[
            pltpu.VMEM((QUERY_BLOCKS, HD, STACK), F32),
            pltpu.VMEM((KEY_BLOCKS * BLK, HD), F32),
            pltpu.VMEM((KEY_BLOCKS * BLK, HD), F32),
        ],
        compiler_params=params(),
        name="back_tiles",
    )(places, plan, stats, keys, vals, qs, gs)
    slice_width = width // (nl * NC)
    w_split = w_key.reshape(2, 2, NC, slice_width, HD)
    block = (ROWS, HD)
    results = pl.pallas_call(
        reduce_kernel,
        out_shape=(
            shape((ROWS, GROUP * HD), BF16),
            shape((ROWS, HD), BF16),
            shape((ROWS, slice_width), BF16),
            shape((BLK, HD), F32),
        ),
        in_specs=[vmem, vmem, vmem, vmem, hbm],
        out_specs=(vmem,) * 4,
        scratch_shapes=[
            pltpu.VMEM((4, 2, ROWS + ROWS // 2, HD), BF16),
            pltpu.VMEM((4, 2) + block, BF16),
            pltpu.VMEM((4, 2) + block, BF16),
            pltpu.VMEM((4, 2) + block, BF16),
            pltpu.VMEM((NX - 1, ROWS, GROUP * HD), BF16),
            pltpu.VMEM((NZ, NY - 1, BLK, HD), BF16),
            pltpu.VMEM((2,) + block, BF16),
            pltpu.VMEM((2,) + block, BF16),
            pltpu.VMEM((NX,) + block, BF16),
            pltpu.VMEM((3,) + block, BF16),
            pltpu.VMEM((NX, NZ, NY, BLK, ROWS), BF16),
            pltpu.VMEM((4, 2, slice_width, HD), BF16),
            pltpu.VMEM((NZ, NY, BLK, HD), BF16),
            pltpu.VMEM((ROWS, slice_width), BF16),
            pltpu.VMEM((ROWS, slice_width), BF16),
            pltpu.VMEM((BLK, HD), F32),
            pltpu.VMEM((BLK, HD), F32),
            dma(32), dma(32), dma(2 * (NY - 1)), dma(2 * (NY - 1)), dma(9), dma(9), dma(3), dma(3),
            dma(7), dma(7), dma(2),
        ],
        compiler_params=params(3),
        name="reduce_grads",
    )(dq, dk.reshape(NZ, NY, ROWS, HD), dv.reshape(NZ, NY, ROWS, HD), turned, in_hbm(w_split))
    return pl.pallas_call(
        hand_over_kernel,
        out_shape=tuple(shape(r.shape, r.dtype) for r in results),
        in_specs=[vmem] * 4,
        out_specs=(hbm,) * 4,
        scratch_shapes=[dma(4)],
        compiler_params=params(),
        name="hand_over",
    )(*results)


def solution(mesh):
    nl = mesh.shape["tensor"] // NC
    return jax.shard_map(
        functools.partial(on_device, nl),
        mesh=mesh,
        in_specs=(
            P("dp", None),
            P(None, "tensor"),
            P("dp", "tensor"),
            P("dp", "tensor"),
            P("dp", "tensor"),
            P(),
            P("dp"),
        ),
        out_specs=(P("dp", "tensor"), P("dp", "tensor"), P("dp", "tensor"), P("dp", "tensor")),
        check_vma=False,
    )
```

time: 97.7 us -> 89.7 us (0.918)
  the two profiles are of different devices: /device:TPU:2 before, /device:TPU:64 now
where the time goes in v3:
time: 89.7 us; the launch traced here: 89.5 us
  Pallas kernels  88.8 us (99%)
    pallas_call x1, Pallas kernels, on_device(): pl.pallas_call(reduce_kernel, out_shape=(shape((ROWS, GROUP * HD), BF16),...  36.5 us
    pallas_call x1, Pallas kernels, on_device(): pl.pallas_call(gather_kernel, out_shape=(shape((NZ, NY, ROWS, HD), BF16),...  30.6 us
    pallas_call x1, Pallas kernels, on_device(): pl.pallas_call(back_kernel, out_shape=(shape((NX, ROWS, GROUP * HD), BF16...  7.67 us
    pallas_call x1, Pallas kernels, on_device(): pl.pallas_call(share_kernel, out_shape=shape((3, QUERY_BLOCKS, STACK), F3...  7.11 us
    pallas_call x1, Pallas kernels, on_device(): pl.pallas_call(stats_kernel, out_shape=(shape((3, QUERY_BLOCKS, STACK), F...  6.27 us

profile of v3, /device:TPU:64, one launch (start us, length us, event | category | flops | bytes accessed | tf_op | source)
XLA Modules:
  0.0 89.5 jit_solution(7047787560022448793)
XLA Ops:
  0.6 30.6 %gather_rows.1 = (bf16[2,8,128,128]{3,2,1,0:T(8,128)(2,1)S(1)}, bf16[2,8,144,128]{3,2,1,0:T(8,128)(2,1)S(1)}, bf16[4,128,512]{2,1,0:T(8,128)(2,1)S(1)}, bf16[4,1...) custom-call(bf16[128,4096]{1,0:T(8,128)(2,1)} %inputs.1, ...), custom_call_target="tpu_custom_call" | custom-call | tf_op jit(solution)/shard_map/gather_rows/pallas_call | solution.py:631
  31.2 6.3 %row_stats.1 = (f32[3,8,256]{2,1,0:T(8,128)S(1)}, s32[512]{0:T(512)S(1)}) custom-call(s32[8,128]{1,0:T(8,128)S(1)} %get-tuple-element.19.places, bf16[2048,128]{1,0:T(8,128)(2,1)S(1)} %bitcast.7, bf16[16,144,128]{2,1,0:T(8,128)(2,1)S(1)} %bitcast.5, bf16[4,128,512]{2,1,0:T(8,128)(2,1)S(1)} %get-tuple-element.22.qs, bf16[4,144,512]{2,1,0:T(8,128)(2,1)S(1)} %get-tuple-element.23.gs), custom_call_target="tpu_custom_call" | custom-call | tf_op jit(solution)/shard_map/row_stats/pallas_call | solution.py:655
  37.5 7.1 %share_stats.1.stats = f32[3,8,256]{2,1,0:T(8,128)S(1)} custom-call(f32[3,8,256]{2,1,0:T(8,128)S(1)} %get-tuple-element.25.stats), custom_call_target="tpu_custom_call" | custom-call | tf_op jit(solution)/shard_map/share_stats/pallas_call | solution.py:664
  44.6 7.7 %back_tiles.1 = (bf16[4,128,512]{2,1,0:T(8,128)(2,1)S(1)}, bf16[2048,128]{1,0:T(8,128)(2,1)S(1)}, bf16[2048,128]{1,0:T(8,128)(2,1)S(1)}) custom-call(s32[8,128]{1,0:T(8,128)S(1)} %get-tuple-element.19.places, s32[512]{0:T(512)S(1)} %get-tuple-element.24.plan, f32[3,8,256]{2,1,0:T(8,128)S(1)} %share_stats.1.stats, bf16[2048,128]{1,0:T(8,128)(2,1)S(1)} %bitcast.8, ...), custom_call_target="tpu_custom_call" | custom-call | tf_op jit(solution)/shard_map/back_tiles/pallas_call | solution.py:675
  52.3 36.5 %reduce_grads.1 = (bf16[128,512]{1,0:T(8,128)(2,1)S(1)}, bf16[128,128]{1,0:T(8,128)(2,1)S(1)}, bf16[128,512]{1,0:T(8,128)(2,1)S(1)}, f32[64,128]{1,0:T(8,128)S(1)}) custom-call(bf16[4,128,512]{2,1,0:T(8,128)(2,1)S(1)} %get-tuple-element.26.dq, bf16[2,8,128,128]{3,2,1,0:T(8,128)(2,1)S(1)} %bitcast.9, bf16[2,8,128,128]{3,2,1,0:T(8,128)(2,1)S(1)} %bitcast.10, ...), custom_call_target="tpu_custom_call" | custom-call | tf_op jit(solution)/shard_map/reduce_grads/pallas_call | solution.py:695
  88.8 0.7 hand_over.1

commit v4 on v3

--- a/solution.py
+++ b/solution.py
@@ -18,7 +18,7 @@
 STACK = GROUP * BLK
 CHUNK = 4
 CHUNKS = KEY_BLOCKS // CHUNK
-SIDE = 2
+SIDE = 4
 PARTS = 4
 LIST, COUNTS, ITEMS, TOTAL, PLAN = 40, 320, 336, 416, 512
 SCALE = 1.0 / math.sqrt(HD)
@@ -46,6 +46,13 @@
 
 def device(y, zh, x, tensor):
     return ((y * NZ + zh) * NX + x, tensor)
+
+
+def quad_of(y, zh, x, zl, core):
+    quarter = rem(zl, 2)
+    near = zl + 1 - 2 * quarter
+    places = ((zl, 1 - core), (near, core), (near, 1 - core))
+    return quarter, [device(y, zh, x, chip * NC + c) for chip, c in places]
 
 
 def greet(peers):
@@ -102,15 +109,18 @@
 
 
 def gather_kernel(
-    inputs, w_key, values, queries, d_out, doc_lens, block_pos, keys, vals, qs, gs, turned, places,
-    x_buf, w_buf, docs, pos, y_send, y_recv, x_send, x_recv, z_send, z_recv, load_sem,
+    inputs, w_key, w_split, values, queries, d_out, doc_lens, block_pos,
+    keys, vals, qs, gs, turned, w_all, places,
+    x_buf, w_buf, docs, pos, y_send, y_recv, x_send, x_recv, z_send, z_recv, s_send, s_recv, load_sem,
 ):
     y, zh, x, t = place()
     ups = [device(rem(y + j, NY), zh, x, t) for j in (1, 2)]
     downs = [device(rem(y + NY - j, NY), zh, x, t) for j in (1, 2)]
     others_x = [device(y, zh, rem(x + j, NX), t) for j in range(1, NX)]
     partner = device(y, 1 - zh, x, t)
-    peers = [partner] + ups + downs + others_x
+    zl, core = lax.div(t, jnp.int32(NC)), rem(t, NC)
+    quarter, quad = quad_of(y, zh, x, zl, core)
+    peers = [partner] + ups + downs + others_x + quad[:2]
     greet(peers)
     loads = [
         pltpu.make_async_copy(src, dst, load_sem.at[i])
@@ -121,6 +131,7 @@
                 (d_out, gs.at[x, pl.ds(0, ROWS)]),
                 (queries, qs.at[x]),
                 (doc_lens, docs),
+                (w_split.at[:, quarter, core], w_all.at[0]),
             )
         )
     ]
@@ -129,10 +140,10 @@
     for i in range(PARTS):
         cut = slice(i * depth, (i + 1) * depth)
         parts.append((
-            pltpu.make_async_copy(w_key.at[cut], w_buf.at[cut], load_sem.at[5 + 2 * i]),
-            pltpu.make_async_copy(inputs.at[:, cut], x_buf.at[:, cut], load_sem.at[6 + 2 * i]),
+            pltpu.make_async_copy(w_key.at[cut], w_buf.at[cut], load_sem.at[6 + 2 * i]),
+            pltpu.make_async_copy(inputs.at[:, cut], x_buf.at[:, cut], load_sem.at[7 + 2 * i]),
         ))
-    for load in loads + [load for pair in parts for load in pair]:
+    for load in loads[:5] + [load for pair in parts for load in pair] + loads[5:]:
         load.start()
     loads[0].wait()
     lane = lax.broadcasted_iota(jnp.int32, (16, ROWS), 1)
@@ -143,32 +154,6 @@
     vals[zh, y, ROWS : ROWS + 16, :] = mine.astype(F32).astype(BF16)
     gs[x, ROWS : ROWS + 16, 0:HD] = here.astype(F32).astype(BF16)
     gs[x, ROWS : ROWS + 16, HD:] = jnp.zeros((16, (GROUP - 1) * HD), BF16)
-    loads[1].wait()
-    meet(peers)
-
-    y_sems, x_sems, z_sems = (y_send, y_recv), (x_send, x_recv), (z_send, z_recv)
-
-    def half_k(ref, way):
-        return ref.at[pl.ds(way * 64, 64)]
-
-    def half_v(ref, way):
-        return ref.at[pl.ds(0, 64)] if way == 0 else ref.at[pl.ds(64, ROWS + 16 - 64)]
-
-    def tree(arr, half, z, base):
-        return Tree(lambda o: arr.at[z, o], half, y, NY, ups, downs, y_sems, base)
-
-    v_own, k_own = tree(vals, half_v, zh, 0), tree(keys, half_k, zh, 8)
-    v_far, k_far = tree(vals, half_v, 1 - zh, 16), tree(keys, half_k, 1 - zh, 24)
-
-    z_v = send(vals.at[zh, y], vals.at[zh, y], z_sems, 0, partner)
-    v_own.first()
-    sideways = []
-    loads[2].wait()
-    for j in (2, 1, 3):
-        sideways.append(send(gs.at[x], gs.at[x], x_sems, j - 1, others_x[j - 1]))
-    loads[3].wait()
-    for j in (2, 1, 3):
-        sideways.append(send(qs.at[x], qs.at[x], x_sems, j + 2, others_x[j - 1]))
     projected = jnp.zeros((ROWS, HD), F32)
     for i, pair in enumerate(parts):
         cut = slice(i * depth, (i + 1) * depth)
@@ -178,8 +163,33 @@
             x_buf[:, cut], w_buf[cut, :], preferred_element_type=F32
         )
     keys[zh, y] = projected.astype(BF16)
+    for load in loads[1:4]:
+        load.wait()
+    meet(peers)
+
+    y_sems, x_sems, z_sems = (y_send, y_recv), (x_send, x_recv), (z_send, z_recv)
+
+    def half_k(ref, way):
+        return ref.at[pl.ds(way * 64, 64)]
+
+    def half_v(ref, way):
+        return ref.at[pl.ds(0, 64)] if way == 0 else ref.at[pl.ds(64, ROWS + 16 - 64)]
+
+    def tree(arr, half, z, base):
+        return Tree(lambda o: arr.at[z, o], half, y, NY, ups, downs, y_sems, base)
+
+    v_own, k_own = tree(vals, half_v, zh, 0), tree(keys, half_k, zh, 8)
+    v_far, k_far = tree(vals, half_v, 1 - zh, 16), tree(keys, half_k, 1 - zh, 24)
+
     z_k = send(keys.at[zh, y], keys.at[zh, y], z_sems, 1, partner)
+    z_v = send(vals.at[zh, y], vals.at[zh, y], z_sems, 0, partner)
     k_own.first()
+    v_own.first()
+    right, left = others_x[0], others_x[-1]
+    sideways = []
+    for i, (arr, _) in enumerate(((gs, half_v), (qs, half_k))):
+        for way, peer in enumerate((right, left)):
+            sideways.append(send(arr.at[x], arr.at[x], x_sems, 2 * i + way, peer))
 
     def turn(first, last):
         def body(j, carry):
@@ -195,22 +205,38 @@
         lax.fori_loop(first, last, body, 0)
 
     tiles = inputs.shape[1] // 128
+    onward = []
+
+    def pass_on(i, arr, half):
+        for way, peer in enumerate((right, left)):
+            sideways[2 * i + way].wait_recv()
+            ref = half(arr.at[rem(x + (NX - 1 if way == 0 else 1), NX)], way)
+            onward.append(send(ref, ref, x_sems, 4 + 2 * i + way, peer))
+
     turn(0, tiles // 4)
+    k_own.second()
     v_own.second()
+    z_k.wait_recv()
+    k_far.first()
     z_v.wait_recv()
     v_far.first()
-    k_own.second()
-    z_k.wait_recv()
-    k_far.first()
+    sides = ((quarter, 1 - core), (1 - quarter, core))
+    swaps = [
+        send(w_split.at[:, q, c], w_all.at[j + 1], (s_send, s_recv), j, quad[j])
+        for j, (q, c) in enumerate(sides)
+    ]
+    pass_on(0, gs, half_v)
     turn(tiles // 4, tiles // 2)
+    k_far.second()
+    pass_on(1, qs, half_k)
     v_far.second()
-    k_far.second()
     turn(tiles // 2, tiles)
     loads[4].wait()
+    loads[5].wait()
     rings = (v_own, k_own, v_far, k_far)
     for r in rings:
         r.end()
-    for copy in sideways:
+    for copy in onward + swaps:
         copy.wait_recv()
     total = jnp.zeros((16, ROWS), F32)
     for z in range(NZ):
@@ -228,7 +254,7 @@
     z_k.wait_send()
     for r in rings:
         r.drain()
-    for copy in sideways:
+    for copy in sideways + onward + swaps:
         copy.wait_send()
 
 
@@ -242,27 +268,32 @@
 def make_plan(places, plan):
     starts = doc_starts(places)
 
-    def visit(query, items):
-        mine = places[0, KEY_BLOCKS + query]
-        start = jnp.int32(0)
-        for s in starts[1:]:
-            start = jnp.where(s <= mine * BLK, s, start)
-        low = lax.div(start, jnp.int32(BLK))
-        begin = query * LIST
-        count = jnp.int32(0)
+    def visit(pair, items):
+        queries = [pair * 2, pair * 2 + 1]
+        mine = [places[0, KEY_BLOCKS + query] for query in queries]
+        low = []
+        for m in mine:
+            start = jnp.int32(0)
+            for s in starts[1:]:
+                start = jnp.where(s <= m * BLK, s, start)
+            low.append(lax.div(start, jnp.int32(BLK)))
+        at = [query * LIST for query in queries]
         for b in range(KEY_BLOCKS):
             pk = places[0, b]
-            plan[begin + count] = jnp.int32(b)
-            count = count + ((pk <= mine) & (pk >= low)).astype(jnp.int32)
-        for j in range(CHUNK):
-            plan[begin + count + j] = jnp.int32(0)
-        plan[COUNTS + query] = count
-        for c in range(CHUNKS):
-            plan[ITEMS + items] = query * 16 + c
-            items = items + (count > c * CHUNK).astype(jnp.int32)
+            for i in range(2):
+                plan[at[i]] = jnp.int32(b)
+                at[i] = at[i] + ((pk <= mine[i]) & (pk >= low[i])).astype(jnp.int32)
+        for i, query in enumerate(queries):
+            for j in range(CHUNK):
+                plan[at[i] + j] = jnp.int32(0)
+            count = at[i] - query * LIST
+            plan[COUNTS + query] = count
+            for c in range(CHUNKS):
+                plan[ITEMS + items] = query * 16 + c
+                items = items + (count > c * CHUNK).astype(jnp.int32)
         return items
 
-    items = lax.fori_loop(0, QUERY_BLOCKS, visit, jnp.int32(0))
+    items = lax.fori_loop(0, QUERY_BLOCKS // 2, visit, jnp.int32(0))
     plan[ITEMS + items] = jnp.int32(0)
     plan[TOTAL] = items
 
@@ -408,7 +439,7 @@
 
     lax.fori_loop(0, lax.div(plan[TOTAL] + (SIDE - 1), jnp.int32(SIDE)), step, 0)
     for query in range(QUERY_BLOCKS):
-        dq_rows = (dq_sum[query] * SCALE).T.astype(BF16)
+        dq_rows = (dq_sum[query] * SCALE).astype(BF16).T
         rows = slice((query % 2) * BLK, (query % 2 + 1) * BLK)
         for h in range(GROUP):
             dq[query // 2, rows, h * HD : (h + 1) * HD] = dq_rows[h * BLK : (h + 1) * BLK]
@@ -471,10 +502,10 @@
 
 
 def reduce_kernel(
-    dq, dk, dv, turned, w_key, d_query, d_value, d_input, d_wkey,
-    f_far, f_near, f_made, f_last, q_got, w_got, z_out, z_got,
-    kg, kg_quad, xg, w_all, w_part, in_part, in_got, zw_out, zw_got,
-    f_send, f_recv, w_send, w_recv, x_send, x_recv, z_send, z_recv, s_send, s_recv, load_sem,
+    dq, dk, dv, turned, w_all, w_split, d_query, d_value, d_input, d_wkey,
+    k_got, f_far, f_near, f_made, f_last, q_got, w_got, z_out, z_got,
+    kg, kg_quad, xg, w_last, w_part, in_part, in_got, zw_out, zw_got,
+    k_send, k_recv, f_send, f_recv, w_send, w_recv, x_send, x_recv, z_send, z_recv, s_send, s_recv, load_sem,
 ):
     y, zh, x, t = place()
     zl, core = lax.div(t, jnp.int32(NC)), rem(t, NC)
@@ -482,18 +513,14 @@
     ups, downs = others_y[:2], [others_y[-1], others_y[-2]]
     others_x = [device(y, zh, rem(x + j, NX), t) for j in range(1, NX)]
     partner = device(y, 1 - zh, x, t)
-    half, quarter = lax.div(zl, jnp.int32(2)), rem(zl, 2)
-    sibling = device(y, zh, x, zl * NC + 1 - core)
-    across = [device(y, zh, x, (zl + 1 - 2 * quarter) * NC + c) for c in (core, 1 - core)]
-    quad = [sibling] + across
+    half = lax.div(zl, jnp.int32(2))
+    quarter, quad = quad_of(y, zh, x, zl, core)
     over = device(y, zh, x, rem(zl + 2, 4) * NC + core)
     x_sems, z_sems, s_sems = (x_send, x_recv), (z_send, z_recv), (s_send, s_recv)
     peers = [partner] + others_y + others_x + quad + [over]
     greet(peers)
     own_x = pltpu.make_async_copy(turned.at[x], xg.at[x], load_sem.at[0])
-    own_w = pltpu.make_async_copy(w_key.at[:, quarter, core], w_all.at[0], load_sem.at[1])
     own_x.start()
-    own_w.start()
     meet(peers)
 
     def fold(arr, z, i):
@@ -503,54 +530,55 @@
         )
 
     far = 1 - zh
-    k_far, k_own = fold(dk, far, 0), fold(dk, zh, 1)
-    v_far, v_own = fold(dv, far, 2), fold(dv, zh, 3)
-    k_far.first()
-    k_own.first()
+    v_far, v_own = fold(dv, far, 0), fold(dv, zh, 1)
+
+    def straight(i, z):
+        return [
+            send(
+                dk.at[z, rem(y + j, NY)], k_got.at[i, j - 1], (k_send, k_recv), i * (NY - 1) + j - 1,
+                others_y[j - 1],
+            )
+            for j in (4, 3, 5, 2, 6, 1, 7)
+        ]
+
+    def k_total(i, z, copies):
+        for copy in copies:
+            copy.wait_recv()
+        out = dk[z, y].astype(F32)
+        for j in range(NY - 1):
+            out = out + k_got[i, j].astype(F32)
+        return out
+
+    k_far = straight(0, far)
     x_sends = [
         send(turned.at[rem(x + j, NX)], xg.at[x], x_sems, j - 1, others_x[j - 1]) for j in (2, 1, 3)
     ]
-    w_sides = ((quarter, 1 - core), (1 - quarter, core), (1 - quarter, 1 - core))
-    w_swaps = [
-        send(w_key.at[:, q, c], w_all.at[j + 1], s_sems, j, quad[j]) for j, (q, c) in enumerate(w_sides)
-    ]
-    k_far.second()
-    k_own.second()
-    z_out[0] = k_far.total().astype(BF16)
+    w_swap = send(w_split.at[:, 1 - quarter, 1 - core], w_last, s_sems, 4, quad[2])
+    for copy in k_far:
+        copy.wait_send()
+    k_own = straight(1, zh)
+    z_out[0] = k_total(0, far, k_far).astype(BF16)
     z_key = send(z_out.at[0], z_got.at[0], z_sems, 0, partner)
     v_far.first()
     v_own.first()
-    key_sum = k_own.total()
+    key_sum = k_total(1, zh, k_own)
     z_key.wait_recv()
     kg[x] = (key_sum + z_got[0].astype(F32)).astype(BF16)
 
     kg_sends = [send(kg.at[x], kg.at[x], x_sems, 2 + j, others_x[j - 1]) for j in (2, 1, 3)]
-    kg_swaps = [send(kg.at[x], kg_quad.at[j], s_sems, 3 + j, quad[j]) for j in range(3)]
+    kg_swaps = [send(kg.at[x], kg_quad.at[j], s_sems, j, quad[j]) for j in range(3)]
     q_sends = [
         send(dq.at[rem(x + j, NX)], q_got.at[j - 1], x_sems, 5 + j, others_x[j - 1]) for j in (2, 1, 3)
     ]
     v_far.second()
     v_own.second()
-    own_w.wait()
-    for copy in w_swaps + kg_swaps:
-        copy.wait_recv()
-    quad_heads = [kg[x]] + [kg_quad[j] for j in range(3)]
-
-    def in_block(h):
-        out = jnp.zeros((ROWS, w_all.shape[2]), F32)
-        for j, head in enumerate(quad_heads):
-            out = out + lax.dot_general(head, w_all[j, h], NT, preferred_element_type=F32)
-        return out
-
-    in_part[...] = in_block(1 - half).astype(BF16)
-    in_send = send(in_part, in_got, s_sems, 6, over)
-
     own_x.wait()
     for copy in x_sends + kg_sends:
         copy.wait_recv()
     heads = [kg[src] for src in range(NX)]
     w_sends = []
-    for turn, z in enumerate((far, zh)):
+
+    def spread_product(turn, z):
         product = jnp.zeros((NY * BLK, HD), F32)
         for src in range(NX):
             rows = xg[src, z].reshape(NY * BLK, ROWS)
@@ -564,6 +592,8 @@
                 )
             )
 
+    spread_product(0, far)
+
     def w_total(turn):
         for copy in w_sends[turn * (NY - 1) : (turn + 1) * (NY - 1)]:
             copy.wait_recv()
@@ -572,10 +602,25 @@
             out = out + w_got[turn, j].astype(F32)
         return out
 
+    for copy in [w_swap] + kg_swaps:
+        copy.wait_recv()
+    quad_heads = [kg[x]] + [kg_quad[j] for j in range(3)]
+
+    def in_block(h):
+        out = jnp.zeros((ROWS, w_all.shape[2]), F32)
+        for j, head in enumerate(quad_heads):
+            rows = w_all[j, h] if j < 3 else w_last[h]
+            out = out + lax.dot_general(head, rows, NT, preferred_element_type=F32)
+        return out
+
+    in_part[...] = in_block(1 - half).astype(BF16)
+    in_send = send(in_part, in_got, s_sems, 3, over)
+
+    spread_product(1, zh)
     z_out[1] = v_far.total().astype(BF16)
     z_val = send(z_out.at[1], z_got.at[1], z_sems, 1, partner)
     in_sum = in_block(half)
-    zw_out[...] = w_total(0)
+    zw_out[...] = w_total(0).astype(BF16)
     z_w = send(zw_out, zw_got, z_sems, 2, partner)
     q_sum = dq[x].astype(F32)
     for copy in q_sends:
@@ -589,11 +634,11 @@
     d_value[...] = (v_own.total() + z_got[1].astype(F32)).astype(BF16)
     w_sum = w_total(1)
     z_w.wait_recv()
-    d_wkey[...] = w_sum + zw_got[...]
-
-    for f in (k_far, k_own, v_far, v_own):
+    d_wkey[...] = w_sum + zw_got[...].astype(F32)
+
+    for f in (v_far, v_own):
         f.drain()
-    for copy in [z_key, z_val, z_w, in_send] + x_sends + kg_sends + q_sends + w_sends + w_swaps + kg_swaps:
+    for copy in [z_key, z_val, z_w, in_send, w_swap] + k_own + x_sends + kg_sends + q_sends + w_sends + kg_swaps:
         copy.wait_send()
 
 
@@ -628,7 +673,9 @@
     width = inputs.shape[1]
     pairs = NZ * NY
     shape = jax.ShapeDtypeStruct
-    keys, vals, qs, gs, turned, places = pl.pallas_call(
+    slice_width = width // (nl * NC)
+    w_split = w_key.reshape(2, 2, NC, slice_width, HD)
+    keys, vals, qs, gs, turned, w_all, places = pl.pallas_call(
         gather_kernel,
         out_shape=(
             shape((NZ, NY, ROWS, HD), BF16),
@@ -636,20 +683,21 @@
             shape((NX, ROWS, GROUP * HD), BF16),
             shape((NX, ROWS + 16, GROUP * HD), BF16),
             shape((NX, NZ, NY, BLK, ROWS), BF16),
+            shape((3, 2, slice_width, HD), BF16),
             shape((8, ROWS), jnp.int32),
         ),
-        in_specs=[hbm] * 7,
-        out_specs=(vmem,) * 6,
+        in_specs=[hbm] * 8,
+        out_specs=(vmem,) * 7,
         scratch_shapes=[
             pltpu.VMEM((ROWS, width), BF16),
             pltpu.VMEM((width, HD), BF16),
             pltpu.SMEM((4,), jnp.int32),
             pltpu.SMEM((2,), jnp.int32),
-            dma(32), dma(32), dma(6), dma(6), dma(2), dma(2), dma(5 + 2 * PARTS),
+            dma(32), dma(32), dma(8), dma(8), dma(2), dma(2), dma(2), dma(2), dma(6 + 2 * PARTS),
         ],
         compiler_params=params(1),
         name="gather_rows",
-    )(*(in_hbm(a) for a in (inputs, w_key, values, queries, d_out, doc_lens, block_pos)))
+    )(*(in_hbm(a) for a in (inputs, w_key, w_split, values, queries, d_out, doc_lens, block_pos)))
     keys = keys.reshape(KEY_BLOCKS * BLK, HD)
     vals = vals.reshape(pairs, ROWS + 16, HD)
     stats, plan = pl.pallas_call(
@@ -689,8 +737,6 @@
         compiler_params=params(),
         name="back_tiles",
     )(places, plan, stats, keys, vals, qs, gs)
-    slice_width = width // (nl * NC)
-    w_split = w_key.reshape(2, 2, NC, slice_width, HD)
     block = (ROWS, HD)
     results = pl.pallas_call(
         reduce_kernel,
@@ -700,13 +746,14 @@
             shape((ROWS, slice_width), BF16),
             shape((BLK, HD), F32),
         ),
-        in_specs=[vmem, vmem, vmem, vmem, hbm],
+        in_specs=[vmem] * 5 + [hbm],
         out_specs=(vmem,) * 4,
         scratch_shapes=[
-            pltpu.VMEM((4, 2, ROWS + ROWS // 2, HD), BF16),
-            pltpu.VMEM((4, 2) + block, BF16),
-            pltpu.VMEM((4, 2) + block, BF16),
-            pltpu.VMEM((4, 2) + block, BF16),
+            pltpu.VMEM((NZ, NY - 1) + block, BF16),
+            pltpu.VMEM((2, 2, ROWS + ROWS // 2, HD), BF16),
+            pltpu.VMEM((2, 2) + block, BF16),
+            pltpu.VMEM((2, 2) + block, BF16),
+            pltpu.VMEM((2, 2) + block, BF16),
             pltpu.VMEM((NX - 1, ROWS, GROUP * HD), BF16),
             pltpu.VMEM((NZ, NY - 1, BLK, HD), BF16),
             pltpu.VMEM((2,) + block, BF16),
@@ -714,18 +761,18 @@
             pltpu.VMEM((NX,) + block, BF16),
             pltpu.VMEM((3,) + block, BF16),
             pltpu.VMEM((NX, NZ, NY, BLK, ROWS), BF16),
-            pltpu.VMEM((4, 2, slice_width, HD), BF16),
+            pltpu.VMEM((2, slice_width, HD), BF16),
             pltpu.VMEM((NZ, NY, BLK, HD), BF16),
             pltpu.VMEM((ROWS, slice_width), BF16),
             pltpu.VMEM((ROWS, slice_width), BF16),
-            pltpu.VMEM((BLK, HD), F32),
-            pltpu.VMEM((BLK, HD), F32),
-            dma(32), dma(32), dma(2 * (NY - 1)), dma(2 * (NY - 1)), dma(9), dma(9), dma(3), dma(3),
-            dma(7), dma(7), dma(2),
+            pltpu.VMEM((BLK, HD), BF16),
+            pltpu.VMEM((BLK, HD), BF16),
+            dma(2 * (NY - 1)), dma(2 * (NY - 1)), dma(16), dma(16), dma(2 * (NY - 1)), dma(2 * (NY - 1)), dma(9), dma(9), dma(3), dma(3),
+            dma(5), dma(5), dma(1),
         ],
         compiler_params=params(3),
         name="reduce_grads",
-    )(dq, dk.reshape(NZ, NY, ROWS, HD), dv.reshape(NZ, NY, ROWS, HD), turned, in_hbm(w_split))
+    )(dq, dk.reshape(NZ, NY, ROWS, HD), dv.reshape(NZ, NY, ROWS, HD), turned, w_all, in_hbm(w_split))
     return pl.pallas_call(
         hand_over_kernel,
         out_shape=tuple(shape(r.shape, r.dtype) for r in results),

time: 89.7 us -> 88.4 us (0.986)
  the two profiles are of different devices: /device:TPU:64 before, /device:TPU:1 now
where the time goes in v4:
time: 88.4 us; the launch traced here: 88.2 us
  Pallas kernels  87.5 us (99%)
    pallas_call x1, Pallas kernels, on_device(): pl.pallas_call(reduce_kernel, out_shape=(shape((ROWS, GROUP * HD), BF16),...  40 us
    pallas_call x1, Pallas kernels, on_device(): pl.pallas_call(gather_kernel, out_shape=(shape((NZ, NY, ROWS, HD), BF16),...  29.9 us
    pallas_call x1, Pallas kernels, on_device(): pl.pallas_call(share_kernel, out_shape=shape((3, QUERY_BLOCKS, STACK), F3...  6.57 us
    pallas_call x1, Pallas kernels, on_device(): pl.pallas_call(back_kernel, out_shape=(shape((NX, ROWS, GROUP * HD), BF16...  5.66 us
    pallas_call x1, Pallas kernels, on_device(): pl.pallas_call(stats_kernel, out_shape=(shape((3, QUERY_BLOCKS, STACK), F...  4.63 us

profile of v4, /device:TPU:1, one launch (start us, length us, event | category | flops | bytes accessed | tf_op | source)
XLA Modules:
  0.0 88.2 jit_solution(2832119276130656119)
XLA Ops:
  0.6 29.9 %gather_rows.1 = (bf16[2,8,128,128]{3,2,1,0:T(8,128)(2,1)S(1)}, bf16[2,8,144,128]{3,2,1,0:T(8,128)(2,1)S(1)}, bf16[4,128,512]{2,1,0:T(8,128)(2,1)S(1)}, bf16[4,1...) custom-call(bf16[128,4096]{1,0:T(8,128)(2,1)} %inputs.1, ...), custom_call_target="tpu_custom_call" | custom-call | tf_op jit(solution)/shard_map/gather_rows/pallas_call | solution.py:678
  30.6 4.6 %row_stats.1 = (f32[3,8,256]{2,1,0:T(8,128)S(1)}, s32[512]{0:T(512)S(1)}) custom-call(s32[8,128]{1,0:T(8,128)S(1)} %get-tuple-element.20.places, bf16[2048,128]{1,0:T(8,128)(2,1)S(1)} %bitcast.7, bf16[16,144,128]{2,1,0:T(8,128)(2,1)S(1)} %bitcast.5, bf16[4,128,512]{2,1,0:T(8,128)(2,1)S(1)} %get-tuple-element.23.qs, bf16[4,144,512]{2,1,0:T(8,128)(2,1)S(1)} %get-tuple-element.24.gs), custom_call_target="tpu_custom_call" | custom-call | tf_op jit(solution)/shard_map/row_stats/pallas_call | solution.py:703
  35.2 6.6 %share_stats.1.stats = f32[3,8,256]{2,1,0:T(8,128)S(1)} custom-call(f32[3,8,256]{2,1,0:T(8,128)S(1)} %get-tuple-element.26.stats), custom_call_target="tpu_custom_call" | custom-call | tf_op jit(solution)/shard_map/share_stats/pallas_call | solution.py:712
  41.8 5.7 %back_tiles.1 = (bf16[4,128,512]{2,1,0:T(8,128)(2,1)S(1)}, bf16[2048,128]{1,0:T(8,128)(2,1)S(1)}, bf16[2048,128]{1,0:T(8,128)(2,1)S(1)}) custom-call(s32[8,128]{1,0:T(8,128)S(1)} %get-tuple-element.20.places, s32[512]{0:T(512)S(1)} %get-tuple-element.25.plan, f32[3,8,256]{2,1,0:T(8,128)S(1)} %share_stats.1.stats, bf16[2048,128]{1,0:T(8,128)(2,1)S(1)} %bitcast.8, ...), custom_call_target="tpu_custom_call" | custom-call | tf_op jit(solution)/shard_map/back_tiles/pallas_call | solution.py:723
  47.4 40.0 %reduce_grads.1 = (bf16[128,512]{1,0:T(8,128)(2,1)S(1)}, bf16[128,128]{1,0:T(8,128)(2,1)S(1)}, bf16[128,512]{1,0:T(8,128)(2,1)S(1)}, f32[64,128]{1,0:T(8,128)S(1)}) custom-call(bf16[4,128,512]{2,1,0:T(8,128)(2,1)S(1)} %get-tuple-element.27.dq, bf16[2,8,128,128]{3,2,1,0:T(8,128)(2,1)S(1)} %bitcast.9, bf16[2,8,128,128]{3,2,1,0:T(8,128)(2,1)S(1)} %bitcast.10, ...), custom_call_target="tpu_custom_call" | custom-call | tf_op jit(solution)/shard_map/reduce_grads/pallas_call | solution.py:741
  87.4 0.7 hand_over.1

commit v5 on v4

--- a/solution.py
+++ b/solution.py
@@ -18,7 +18,7 @@
 STACK = GROUP * BLK
 CHUNK = 4
 CHUNKS = KEY_BLOCKS // CHUNK
-SIDE = 4
+SIDE, WIDE = 4, 8
 PARTS = 4
 LIST, COUNTS, ITEMS, TOTAL, PLAN = 40, 320, 336, 416, 512
 SCALE = 1.0 / math.sqrt(HD)
@@ -294,7 +294,8 @@
         return items
 
     items = lax.fori_loop(0, QUERY_BLOCKS // 2, visit, jnp.int32(0))
-    plan[ITEMS + items] = jnp.int32(0)
+    for j in range(SIDE):
+        plan[ITEMS + items + j] = jnp.int32(0)
     plan[TOTAL] = items
 
 
@@ -334,6 +335,23 @@
     )
 
 
+def over_items(plan, step):
+    total = plan[TOTAL]
+    wide = lax.div(total, jnp.int32(WIDE))
+    rest = lax.div(total - wide * WIDE + (SIDE - 1), jnp.int32(SIDE))
+
+    def wide_step(i, carry):
+        step(i * WIDE, WIDE)
+        return carry
+
+    def side_step(i, carry):
+        step(wide * WIDE + i * SIDE, SIDE)
+        return carry
+
+    lax.fori_loop(0, wide, wide_step, 0)
+    lax.fori_loop(0, rest, side_step, 0)
+
+
 def head_stack(ref, query):
     rows = pl.ds(pl.multiple_of((query & 1) * BLK, BLK), BLK)
     return jnp.concatenate(
@@ -349,10 +367,10 @@
         kept[c, 1] = jnp.zeros((QUERY_BLOCKS, STACK), F32)
         kept[c, 2] = jnp.zeros((QUERY_BLOCKS, STACK), F32)
 
-    def step(i, carry):
+    def step(first, width):
         found = []
-        for part in range(SIDE):
-            item = item_of(places, plan, starts, i * SIDE + part)
+        for part in range(width):
+            item = item_of(places, plan, starts, first + part)
             k, v, term, _ = key_chunk(places, plan, item, keys, vals)
             q, g = head_stack(qs, item[0]), head_stack(gs, item[0])
             score = lax.dot_general(k, q, NT, preferred_element_type=F32) * LOG2 + term
@@ -366,9 +384,8 @@
             slot = jnp.where(item[2], item[1], CHUNKS)
             for j, value in enumerate((top, mass, weighted)):
                 kept[slot, j, pl.ds(item[0], 1), :] = value
-        return carry
-
-    lax.fori_loop(0, lax.div(plan[TOTAL] + (SIDE - 1), jnp.int32(SIDE)), step, 0)
+
+    over_items(plan, step)
     top = kept[0, 0]
     for c in range(1, CHUNKS):
         top = jnp.maximum(top, kept[c, 0])
@@ -413,10 +430,10 @@
     dk_sum[...] = jnp.zeros_like(dk_sum)
     dv_sum[...] = jnp.zeros_like(dv_sum)
 
-    def step(i, carry):
+    def step(first, width):
         found = []
-        for part in range(SIDE):
-            item = item_of(places, plan, starts, i * SIDE + part)
+        for part in range(width):
+            item = item_of(places, plan, starts, first + part)
             query = item[0]
             k, v, term, blocks = key_chunk(places, plan, item, keys, vals)
             q, g = head_stack(qs, query), head_stack(gs, query)
@@ -435,9 +452,8 @@
                 rows = pl.ds(pl.multiple_of(b * BLK, BLK), BLK)
                 dv_sum[rows, :] += dv_part[j * BLK : (j + 1) * BLK]
                 dk_sum[rows, :] += dk_part[j * BLK : (j + 1) * BLK]
-        return carry
-
-    lax.fori_loop(0, lax.div(plan[TOTAL] + (SIDE - 1), jnp.int32(SIDE)), step, 0)
+
+    over_items(plan, step)
     for query in range(QUERY_BLOCKS):
         dq_rows = (dq_sum[query] * SCALE).astype(BF16).T
         rows = slice((query % 2) * BLK, (query % 2 + 1) * BLK)

time: 88.4 us -> 86.3 us (0.976)
  the two profiles are of different devices: /device:TPU:1 before, /device:TPU:64 now
where the time goes in v5:
time: 86.3 us; the launch traced here: 86.1 us
  Pallas kernels  85.4 us (99%)
    pallas_call x1, Pallas kernels, on_device(): pl.pallas_call(reduce_kernel, out_shape=(shape((ROWS, GROUP * HD), BF16),...  36.5 us
    pallas_call x1, Pallas kernels, on_device(): pl.pallas_call(gather_kernel, out_shape=(shape((NZ, NY, ROWS, HD), BF16),...  31 us
    pallas_call x1, Pallas kernels, on_device(): pl.pallas_call(share_kernel, out_shape=shape((3, QUERY_BLOCKS, STACK), F3...  7.09 us
    pallas_call x1, Pallas kernels, on_device(): pl.pallas_call(back_kernel, out_shape=(shape((NX, ROWS, GROUP * HD), BF16...  5.48 us
    pallas_call x1, Pallas kernels, on_device(): pl.pallas_call(stats_kernel, out_shape=(shape((3, QUERY_BLOCKS, STACK), F...  4.54 us

profile of v5, /device:TPU:64, one launch (start us, length us, event | category | flops | bytes accessed | tf_op | source)
XLA Modules:
  0.0 86.1 jit_solution(1045556868540934990)
XLA Ops:
  0.6 31.0 %gather_rows.1 = (bf16[2,8,128,128]{3,2,1,0:T(8,128)(2,1)S(1)}, bf16[2,8,144,128]{3,2,1,0:T(8,128)(2,1)S(1)}, bf16[4,128,512]{2,1,0:T(8,128)(2,1)S(1)}, bf16[4,1...) custom-call(bf16[128,4096]{1,0:T(8,128)(2,1)} %inputs.1, ...), custom_call_target="tpu_custom_call" | custom-call | tf_op jit(solution)/shard_map/gather_rows/pallas_call | solution.py:694
  31.7 4.5 %row_stats.1 = (f32[3,8,256]{2,1,0:T(8,128)S(1)}, s32[512]{0:T(512)S(1)}) custom-call(s32[8,128]{1,0:T(8,128)S(1)} %get-tuple-element.20.places, bf16[2048,128]{1,0:T(8,128)(2,1)S(1)} %bitcast.7, bf16[16,144,128]{2,1,0:T(8,128)(2,1)S(1)} %bitcast.5, bf16[4,128,512]{2,1,0:T(8,128)(2,1)S(1)} %get-tuple-element.23.qs, bf16[4,144,512]{2,1,0:T(8,128)(2,1)S(1)} %get-tuple-element.24.gs), custom_call_target="tpu_custom_call" | custom-call | tf_op jit(solution)/shard_map/row_stats/pallas_call | solution.py:719
  36.2 7.1 %share_stats.1.stats = f32[3,8,256]{2,1,0:T(8,128)S(1)} custom-call(f32[3,8,256]{2,1,0:T(8,128)S(1)} %get-tuple-element.26.stats), custom_call_target="tpu_custom_call" | custom-call | tf_op jit(solution)/shard_map/share_stats/pallas_call | solution.py:728
  43.3 5.5 %back_tiles.1 = (bf16[4,128,512]{2,1,0:T(8,128)(2,1)S(1)}, bf16[2048,128]{1,0:T(8,128)(2,1)S(1)}, bf16[2048,128]{1,0:T(8,128)(2,1)S(1)}) custom-call(s32[8,128]{1,0:T(8,128)S(1)} %get-tuple-element.20.places, s32[512]{0:T(512)S(1)} %get-tuple-element.25.plan, f32[3,8,256]{2,1,0:T(8,128)S(1)} %share_stats.1.stats, bf16[2048,128]{1,0:T(8,128)(2,1)S(1)} %bitcast.8, ...), custom_call_target="tpu_custom_call" | custom-call | tf_op jit(solution)/shard_map/back_tiles/pallas_call | solution.py:739
  48.8 36.5 %reduce_grads.1 = (bf16[128,512]{1,0:T(8,128)(2,1)S(1)}, bf16[128,128]{1,0:T(8,128)(2,1)S(1)}, bf16[128,512]{1,0:T(8,128)(2,1)S(1)}, f32[64,128]{1,0:T(8,128)S(1)}) custom-call(bf16[4,128,512]{2,1,0:T(8,128)(2,1)S(1)} %get-tuple-element.27.dq, bf16[2,8,128,128]{3,2,1,0:T(8,128)(2,1)S(1)} %bitcast.9, bf16[2,8,128,128]{3,2,1,0:T(8,128)(2,1)S(1)} %bitcast.10, ...), custom_call_target="tpu_custom_call" | custom-call | tf_op jit(solution)/shard_map/reduce_grads/pallas_call | solution.py:757
  85.3 0.7 hand_over.1

commit v6 on v5

--- a/solution.py
+++ b/solution.py
@@ -519,9 +519,9 @@
 
 def reduce_kernel(
     dq, dk, dv, turned, w_all, w_split, d_query, d_value, d_input, d_wkey,
-    k_got, f_far, f_near, f_made, f_last, q_got, w_got, z_out, z_got,
+    f_far, f_near, f_made, f_last, q_got, w_got, z_out, z_got,
     kg, kg_quad, xg, w_last, w_part, in_part, in_got, zw_out, zw_got,
-    k_send, k_recv, f_send, f_recv, w_send, w_recv, x_send, x_recv, z_send, z_recv, s_send, s_recv, load_sem,
+    f_send, f_recv, w_send, w_recv, x_send, x_recv, z_send, z_recv, s_send, s_recv, load_sem,
 ):
     y, zh, x, t = place()
     zl, core = lax.div(t, jnp.int32(NC)), rem(t, NC)
@@ -548,36 +548,20 @@
     far = 1 - zh
     v_far, v_own = fold(dv, far, 0), fold(dv, zh, 1)
 
-    def straight(i, z):
-        return [
-            send(
-                dk.at[z, rem(y + j, NY)], k_got.at[i, j - 1], (k_send, k_recv), i * (NY - 1) + j - 1,
-                others_y[j - 1],
-            )
-            for j in (4, 3, 5, 2, 6, 1, 7)
-        ]
-
-    def k_total(i, z, copies):
-        for copy in copies:
-            copy.wait_recv()
-        out = dk[z, y].astype(F32)
-        for j in range(NY - 1):
-            out = out + k_got[i, j].astype(F32)
-        return out
-
-    k_far = straight(0, far)
+    k_far, k_own = fold(dk, far, 3), fold(dk, zh, 2)
+    k_far.first()
+    k_own.first()
     x_sends = [
         send(turned.at[rem(x + j, NX)], xg.at[x], x_sems, j - 1, others_x[j - 1]) for j in (2, 1, 3)
     ]
     w_swap = send(w_split.at[:, 1 - quarter, 1 - core], w_last, s_sems, 4, quad[2])
-    for copy in k_far:
-        copy.wait_send()
-    k_own = straight(1, zh)
-    z_out[0] = k_total(0, far, k_far).astype(BF16)
+    k_far.second()
+    k_own.second()
+    z_out[0] = k_far.total().astype(BF16)
     z_key = send(z_out.at[0], z_got.at[0], z_sems, 0, partner)
     v_far.first()
     v_own.first()
-    key_sum = k_total(1, zh, k_own)
+    key_sum = k_own.total()
     z_key.wait_recv()
     kg[x] = (key_sum + z_got[0].astype(F32)).astype(BF16)
 
@@ -652,9 +636,9 @@
     z_w.wait_recv()
     d_wkey[...] = w_sum + zw_got[...].astype(F32)
 
-    for f in (v_far, v_own):
+    for f in (v_far, v_own, k_far, k_own):
         f.drain()
-    for copy in [z_key, z_val, z_w, in_send, w_swap] + k_own + x_sends + kg_sends + q_sends + w_sends + kg_swaps:
+    for copy in [z_key, z_val, z_w, in_send, w_swap] + x_sends + kg_sends + q_sends + w_sends + kg_swaps:
         copy.wait_send()
 
 
@@ -765,11 +749,10 @@
         in_specs=[vmem] * 5 + [hbm],
         out_specs=(vmem,) * 4,
         scratch_shapes=[
-            pltpu.VMEM((NZ, NY - 1) + block, BF16),
-            pltpu.VMEM((2, 2, ROWS + ROWS // 2, HD), BF16),
-            pltpu.VMEM((2, 2) + block, BF16),
-            pltpu.VMEM((2, 2) + block, BF16),
-            pltpu.VMEM((2, 2) + block, BF16),
+            pltpu.VMEM((4, 2, ROWS + ROWS // 2, HD), BF16),
+            pltpu.VMEM((4, 2) + block, BF16),
+            pltpu.VMEM((4, 2) + block, BF16),
+            pltpu.VMEM((4, 2) + block, BF16),
             pltpu.VMEM((NX - 1, ROWS, GROUP * HD), BF16),
             pltpu.VMEM((NZ, NY - 1, BLK, HD), BF16),
             pltpu.VMEM((2,) + block, BF16),
@@ -783,7 +766,7 @@
             pltpu.VMEM((ROWS, slice_width), BF16),
             pltpu.VMEM((BLK, HD), BF16),
             pltpu.VMEM((BLK, HD), BF16),
-            dma(2 * (NY - 1)), dma(2 * (NY - 1)), dma(16), dma(16), dma(2 * (NY - 1)), dma(2 * (NY - 1)), dma(9), dma(9), dma(3), dma(3),
+            dma(32), dma(32), dma(2 * (NY - 1)), dma(2 * (NY - 1)), dma(9), dma(9), dma(3), dma(3),
             dma(5), dma(5), dma(1),
         ],
         compiler_params=params(3),

time: 86.3 us -> 85.8 us (level)
  the two profiles are of different devices: /device:TPU:64 before, /device:TPU:80 now
where the time goes in v6:
time: 85.8 us; the launch traced here: 86 us
  Pallas kernels  85.3 us (99%)
    pallas_call x1, Pallas kernels, on_device(): pl.pallas_call(reduce_kernel, out_shape=(shape((ROWS, GROUP * HD), BF16),...  38.1 us
    pallas_call x1, Pallas kernels, on_device(): pl.pallas_call(gather_kernel, out_shape=(shape((NZ, NY, ROWS, HD), BF16),...  29.4 us
    pallas_call x1, Pallas kernels, on_device(): pl.pallas_call(share_kernel, out_shape=shape((3, QUERY_BLOCKS, STACK), F3...  7.09 us
    pallas_call x1, Pallas kernels, on_device(): pl.pallas_call(back_kernel, out_shape=(shape((NX, ROWS, GROUP * HD), BF16...  5.47 us
    pallas_call x1, Pallas kernels, on_device(): pl.pallas_call(stats_kernel, out_shape=(shape((3, QUERY_BLOCKS, STACK), F...  4.54 us

profile of v6, /device:TPU:80, one launch (start us, length us, event | category | flops | bytes accessed | tf_op | source)
XLA Modules:
  0.0 86.0 jit_solution(64808024469124484)
XLA Ops:
  0.6 29.4 %gather_rows.1 = (bf16[2,8,128,128]{3,2,1,0:T(8,128)(2,1)S(1)}, bf16[2,8,144,128]{3,2,1,0:T(8,128)(2,1)S(1)}, bf16[4,128,512]{2,1,0:T(8,128)(2,1)S(1)}, bf16[4,1...) custom-call(bf16[128,4096]{1,0:T(8,128)(2,1)} %inputs.1, ...), custom_call_target="tpu_custom_call" | custom-call | tf_op jit(solution)/shard_map/gather_rows/pallas_call | solution.py:678
  30.0 4.5 %row_stats.1 = (f32[3,8,256]{2,1,0:T(8,128)S(1)}, s32[512]{0:T(512)S(1)}) custom-call(s32[8,128]{1,0:T(8,128)S(1)} %get-tuple-element.20.places, bf16[2048,128]{1,0:T(8,128)(2,1)S(1)} %bitcast.7, bf16[16,144,128]{2,1,0:T(8,128)(2,1)S(1)} %bitcast.5, bf16[4,128,512]{2,1,0:T(8,128)(2,1)S(1)} %get-tuple-element.23.qs, bf16[4,144,512]{2,1,0:T(8,128)(2,1)S(1)} %get-tuple-element.24.gs), custom_call_target="tpu_custom_call" | custom-call | tf_op jit(solution)/shard_map/row_stats/pallas_call | solution.py:703
  34.6 7.1 %share_stats.1.stats = f32[3,8,256]{2,1,0:T(8,128)S(1)} custom-call(f32[3,8,256]{2,1,0:T(8,128)S(1)} %get-tuple-element.26.stats), custom_call_target="tpu_custom_call" | custom-call | tf_op jit(solution)/shard_map/share_stats/pallas_call | solution.py:712
  41.7 5.5 %back_tiles.1 = (bf16[4,128,512]{2,1,0:T(8,128)(2,1)S(1)}, bf16[2048,128]{1,0:T(8,128)(2,1)S(1)}, bf16[2048,128]{1,0:T(8,128)(2,1)S(1)}) custom-call(s32[8,128]{1,0:T(8,128)S(1)} %get-tuple-element.20.places, s32[512]{0:T(512)S(1)} %get-tuple-element.25.plan, f32[3,8,256]{2,1,0:T(8,128)S(1)} %share_stats.1.stats, bf16[2048,128]{1,0:T(8,128)(2,1)S(1)} %bitcast.8, ...), custom_call_target="tpu_custom_call" | custom-call | tf_op jit(solution)/shard_map/back_tiles/pallas_call | solution.py:723
  47.2 38.1 %reduce_grads.1 = (bf16[128,512]{1,0:T(8,128)(2,1)S(1)}, bf16[128,128]{1,0:T(8,128)(2,1)S(1)}, bf16[128,512]{1,0:T(8,128)(2,1)S(1)}, f32[64,128]{1,0:T(8,128)S(1)}) custom-call(bf16[4,128,512]{2,1,0:T(8,128)(2,1)S(1)} %get-tuple-element.27.dq, bf16[2,8,128,128]{3,2,1,0:T(8,128)(2,1)S(1)} %bitcast.9, bf16[2,8,128,128]{3,2,1,0:T(8,128)(2,1)S(1)} %bitcast.10, ...), custom_call_target="tpu_custom_call" | custom-call | tf_op jit(solution)/shard_map/reduce_grads/pallas_call | solution.py:741
  85.3 0.7 hand_over.1
